TPU v7x, 128 devices: a whole 4x4x4 slice. The times are simulated.
128 devices in a mesh: pipe: 4 (over x), dp: 8 (over y, core), tensor: 4 (over z).
Axes of the slice: x: 4, y: 4, z: 4, core: 2. Of those that a mesh axis runs over, the one named last changes fastest.
Arguments:
- tokens: bfloat16 [4, 2048, 5120], P('pipe', 'dp', 'tensor'), may hold values from -6 to 6
- norm_gain: bfloat16 [4, 5120], P('pipe'), may hold values from 0.099609375 to 1.8984375
- w_query: bfloat16 [4, 5120, 4096], P('pipe', None, 'tensor'), may hold values from -0.078125 to 0.078125
- key_value_weight: bfloat16 [4, 5120, 1024], P('pipe', None, 'tensor'), may hold values from -0.078125 to 0.078125
- w_out: bfloat16 [4, 4096, 5120], P('pipe', 'tensor'), may hold values from -0.5 to 0.5
- cache_kv: bfloat16 [4, 8192, 4, 256], P('pipe', 'dp', 'tensor'), may hold values from -80 to 80
- cache_lengths: int32 [4, 4], P('pipe'), may hold values from 1 to 4096, 8192 in all within a row
- row_lengths: int32 [4, 4], P('pipe'), may hold values from 1 to 1024, 2048 in all within a row
- block_owner: int32 [4, 16, 1], P('pipe'), may hold values from 0 to 7; in each aligned block of 2 rows (0 to 1, 2 to 3, ..., all dimensions but the last counted through in order) no two rows name the same one
Outputs:
- handed: bfloat16 [4, 2048, 5120], P('pipe', 'dp', 'tensor')
- blocks_held: float32 [4, 8], P('pipe', 'dp')
Inputs may be any that keep to these rules, and one draw needn't show every extreme that they name: `block_owner`: the 2 aligned row blocks of one data rank at one section hand at most 1 block to any one data rank. `cache_lengths`: each section's documents hold 8192 cached positions in all; the longest exactly 4096. `row_lengths`: each section's documents hold 2048 rows in all; the longest exactly 1024.
All inputs are finite; a program needn't handle non-finite values.
Results may differ from a plain program's by a relative error of at most 0.012.
The roundings to bfloat16 on the way count: a program that leaves them out, or rounds other values in their place, can miss the bound.
Values may be sent and summed in bfloat16 or wider, within the bound.
A program may use at most 192 MiB of HBM per device.

v0:
```python
import jax
import jax.numpy as jnp
from jax import lax
from jax.sharding import PartitionSpec as P

HEAD_SIZE = 128
BLOCK_ROWS = 128


EPS = 1e-06
NEG = -1e30


def from_behind(block, axis, distance):
    devices = range(lax.axis_size(axis))
    route = [((i - distance) % len(devices), i) for i in devices]
    return lax.ppermute(block, axis, route)


def doc_ids(lengths, amount):
    bounds = jnp.cumsum(lengths)
    places = jnp.arange(amount, dtype=jnp.int32)
    return jnp.sum((places[:, None] >= bounds[None, :]).astype(jnp.int32), axis=1)


def block_loads(row_len, cache_len, amount, block_size):
    row_doc = doc_ids(row_len, amount)
    bounds = jnp.cumsum(row_len)
    starts = bounds - row_len
    offsets = cache_len - starts + 1
    doc_numbers = jnp.arange(row_len.shape[0], dtype=jnp.int32)
    matches = (row_doc[:, None] == doc_numbers[None, :]).astype(jnp.int32)
    per_row = jnp.sum(matches * offsets[None, :], axis=1) + jnp.arange(amount, dtype=jnp.int32)
    return jnp.sum(per_row.reshape(amount // block_size, block_size), axis=1)


def on_device(
    tokens,
    norm_gain,
    w_query,
    key_value_weight,
    w_out,
    cache_kv,
    cache_lengths,
    row_lengths,
    block_owner,
):
    rank_count = lax.axis_size("dp")
    my_rank = lax.axis_index("dp")
    own_rows = tokens[0]
    row_count = own_rows.shape[0]
    blocks_here = row_count // BLOCK_ROWS
    pair_slots = (blocks_here + rank_count - 1) // rank_count
    slot_count = rank_count * pair_slots
    head_width = w_query.shape[2]
    kv_heads = key_value_weight.shape[2] // (2 * HEAD_SIZE)
    group_list = head_width // HEAD_SIZE // kv_heads
    cache_rows = cache_kv.shape[1]
    shard_span = cache_rows + row_count
    cache_doc = doc_ids(cache_lengths[0], cache_rows * rank_count)
    row_doc = doc_ids(row_lengths[0], row_count * rank_count)
    full_rows = lax.all_gather(own_rows, "tensor", axis=1, tiled=True)
    widened = full_rows.astype(jnp.float32)
    factor = lax.rsqrt(jnp.mean(widened * widened, axis=1, keepdims=True) + EPS)
    normed = (widened * factor * norm_gain[0].astype(jnp.float32)).astype(jnp.bfloat16)
    query_rows = jnp.dot(normed, w_query[0], preferred_element_type=jnp.float32).astype(
        jnp.bfloat16
    )
    key_value_rows = jnp.dot(
        normed, key_value_weight[0], preferred_element_type=jnp.float32
    ).astype(jnp.bfloat16)
    owners = block_owner[0, :, 0]
    owner_grid = owners.reshape(rank_count, blocks_here)
    block_ids = jnp.arange(blocks_here, dtype=jnp.int32)
    earlier = block_ids[None, :] < block_ids[:, None]
    same_owner = owner_grid[:, :, None] == owner_grid[:, None, :]
    order_in = jnp.sum((same_owner & earlier[None]).astype(jnp.int32), axis=2)
    mine_owner = lax.dynamic_index_in_dim(owner_grid, my_rank, 0, keepdims=False)
    mine_order = lax.dynamic_index_in_dim(order_in, my_rank, 0, keepdims=False)
    mine_slot = mine_owner * pair_slots + mine_order
    slot_ids = jnp.arange(slot_count, dtype=jnp.int32)
    choose = (mine_slot[:, None] == slot_ids[None, :]).astype(jnp.bfloat16)
    outgoing = jnp.einsum(
        "jr,jqe->rqe",
        choose,
        query_rows.reshape(blocks_here, BLOCK_ROWS, head_width),
        preferred_element_type=jnp.float32,
    ).astype(jnp.bfloat16)
    arrived = lax.all_to_all(outgoing, "dp", split_axis=0, concat_axis=0, tiled=True)
    pair_ids = jnp.arange(pair_slots, dtype=jnp.int32)
    slot_hits = (owner_grid == my_rank)[:, :, None] & (
        order_in[:, :, None] == pair_ids[None, None, :]
    )
    slot_live = jnp.any(slot_hits, axis=1).reshape(slot_count)
    which_block = jnp.sum(slot_hits.astype(jnp.int32) * block_ids[None, :, None], axis=1)
    source_ids = jnp.arange(rank_count, dtype=jnp.int32)
    slot_start = ((source_ids[:, None] * blocks_here + which_block) * BLOCK_ROWS).reshape(
        slot_count
    )
    slot_rows = slot_start[:, None] + jnp.arange(BLOCK_ROWS, dtype=jnp.int32)[None, :]
    slot_docs = jnp.take(row_doc, slot_rows)
    history_rows = jnp.concatenate(
        [cache_kv[0].reshape(cache_rows, kv_heads * 2 * HEAD_SIZE), key_value_rows], axis=0
    )
    start_state = (
        jnp.full((slot_count, BLOCK_ROWS, kv_heads, group_list), NEG, jnp.float32),
        jnp.zeros((slot_count, BLOCK_ROWS, kv_heads, group_list), jnp.float32),
        jnp.zeros((slot_count, BLOCK_ROWS, kv_heads, group_list, HEAD_SIZE), jnp.float32),
    )
    piece = lax.all_gather(history_rows, "dp", axis=0, tiled=True)
    length = piece.shape[0]
    places = jnp.arange(length, dtype=jnp.int32)
    shard_of = places // shard_span
    offset = places - shard_of * shard_span
    in_cache = offset < cache_rows
    cache_index = jnp.clip(shard_of * cache_rows + offset, 0, cache_rows * rank_count - 1)
    row_index = jnp.clip(shard_of * row_count + offset - cache_rows, 0, row_count * rank_count - 1)
    key_doc = jnp.where(in_cache, jnp.take(cache_doc, cache_index), jnp.take(row_doc, row_index))
    key_row = jnp.where(in_cache, -1, row_index)
    shaped = piece.reshape(length, kv_heads, 2 * HEAD_SIZE)
    key_part = shaped[:, :, :HEAD_SIZE]
    value_part = shaped[:, :, HEAD_SIZE:]

    def per_slot(slot_index, carried):
        visible = (slot_docs[slot_index][:, None] == key_doc[None, :]) & (
            key_row[None, :] <= slot_rows[slot_index][:, None]
        )

        def update(carried_in):
            old_max, old_sum, old_acc = carried_in
            query_slot = arrived[slot_index].reshape(BLOCK_ROWS, kv_heads, group_list, HEAD_SIZE)
            scores = jnp.einsum(
                "qkgd,nkd->qkgn", query_slot, key_part, preferred_element_type=jnp.float32
            ) * HEAD_SIZE ** (-0.5)
            visible_wide = visible[:, None, None, :]
            scores = jnp.where(visible_wide, scores, NEG)
            prior = old_max[slot_index]
            newest = jnp.maximum(prior, jnp.max(scores, axis=3))
            weights = jnp.where(visible_wide, jnp.exp(scores - newest[..., None]), 0.0)
            rescale = jnp.exp(prior - newest)
            summed = old_sum[slot_index] * rescale + jnp.sum(weights, axis=3)
            product = jnp.einsum(
                "qkgn,nkd->qkgd",
                weights.astype(jnp.bfloat16),
                value_part,
                preferred_element_type=jnp.float32,
            )
            accrued = old_acc[slot_index] * rescale[..., None] + product
            return (
                old_max.at[slot_index].set(newest),
                old_sum.at[slot_index].set(summed),
                old_acc.at[slot_index].set(accrued),
            )

        def keep_state(carried_in):
            return carried_in

        return lax.cond(slot_live[slot_index] & jnp.any(visible), update, keep_state, carried)

    final_max, final_sum, final_acc = lax.fori_loop(0, slot_count, per_slot, start_state)
    safe_sum = jnp.where(final_sum > 0.0, final_sum, 1.0)
    attended = (
        (final_acc / safe_sum[..., None])
        .astype(jnp.bfloat16)
        .reshape(slot_count, BLOCK_ROWS, head_width)
    )
    splits = lax.axis_size("tensor")
    width_split = w_out.shape[2] // splits
    split_weight = w_out[0].reshape(head_width, splits, width_split)
    by_pair = attended.reshape(rank_count, pair_slots, BLOCK_ROWS, head_width)
    partial_value = jnp.einsum(
        "dpqe,etf->dtpqf", by_pair, split_weight, preferred_element_type=jnp.float32
    ).astype(jnp.bfloat16)
    flat_parts = partial_value.reshape(rank_count * splits * pair_slots, BLOCK_ROWS, width_split)
    came = lax.all_to_all(flat_parts, ("dp", "tensor"), split_axis=0, concat_axis=0, tiled=True)
    came = came.reshape(rank_count, splits, pair_slots, BLOCK_ROWS, width_split)
    reduced = jnp.sum(came.astype(jnp.float32), axis=1).reshape(slot_count, BLOCK_ROWS, width_split)
    summed_rows = jnp.take(reduced, mine_slot, axis=0).reshape(row_count, width_split)
    section_out = (own_rows.astype(jnp.float32) + summed_rows).astype(jnp.bfloat16)
    handed = from_behind(section_out[None], "pipe", 1)
    loads = block_loads(row_lengths[0], cache_lengths[0], row_count * rank_count, BLOCK_ROWS)
    work_sum = jnp.sum((owners == my_rank).astype(jnp.int32) * loads)
    divisor = BLOCK_ROWS * (cache_rows * rank_count // 2 + row_count * rank_count // 2)
    blocks_held = (work_sum.astype(jnp.float32) / jnp.float32(divisor)).reshape(1, 1)
    return (handed, blocks_held)


def solution(mesh):
    placed = (
        P("pipe", "dp", "tensor"),
        P("pipe", None),
        P("pipe", None, "tensor"),
        P("pipe", None, "tensor"),
        P("pipe", "tensor", None),
        P("pipe", "dp", "tensor", None),
        P("pipe", None),
        P("pipe", None),
        P("pipe", None, None),
    )
    return jax.shard_map(
        on_device,
        mesh=mesh,
        in_specs=placed,
        out_specs=(P("pipe", "dp", "tensor"), P("pipe", "dp")),
        check_vma=False,
    )
```

profile of v0, /device:TPU:8, one launch (start us, length us, event | category | flops | bytes accessed | tf_op | source)
XLA Modules:
  0.0 978.0 jit_solution(10741385073910463103)
XLA Ops:
  8.7 38.7 %all-gather.6.cloned.1.call-done = bf16[1,256,5120]{2,1,0:T(8,128)(2,1)} async-done(((bf16[1,256,1280]{2,1,0:T(8,128)(2,1)}), bf16[1,256,5120]{2,1,0:T(8,128)(2,1)}) %all-gather.6.cloned.1.call-update) | async-done | bytes 2621456 | tf_op jit(solution)/shard_map/all_gather | solution.py:62
  56.0 7.7 fusion.62
  67.4 4.8 all-to-all-start
  72.3 6.2 gather_fusion
  78.5 56.8 %gather_fusion.2 = s32[10240]{0:T(1024)S(1)} fusion(s32[2048]{0:T(1024)S(1)} %convert_reduce_fusion.2, s32[10240]{0:T(1024)S(1)} %broadcast_clamp_fusion), kind=kCustom, calls=%fused_computation.2 | custom fusion | bytes 122880 | tf_op jit(solution)/shard_map/jit(_take)/gather | solution.py:118
  135.5 19.4 %reshape_squeeze.11 = bf16[1024,4,1280]{2,1,0:T(4,128)(2,1)} reshape(bf16[1,1024,5120]{2,1,0:T(8,128)(2,1)} %param.23) | data formatting | bytes 20971520 | tf_op jit(solution)/shard_map/reshape;squeeze | solution.py:169
  155.1 56.8 %gather_fusion.1 = s32[10240]{0:T(1024)S(1)} fusion(s32[8192]{0:T(1024)S(1)} %convert_reduce_fusion.1, s32[10240]{0:T(1024)S(1)} %broadcast_clamp_fusion.1), kind=kCustom, calls=%fused_computation.1 | custom fusion | bytes 122880 | tf_op jit(solution)/shard_map/jit(_take)/gather | solution.py:118
  214.5 4.2 fusion.90
  221.2 543.3 %while.21 = (s32[]{:T(128)}, f32[8,128,1,8]{1,3,2,0:T(8,128)S(1)}, f32[8,128,1,8]{1,3,2,0:T(8,128)S(1)}, f32[8,128,1,8,128]{4,1,3,2,0:T(8,128)}, pred[8]{0:T(512...) while((s32[]{:T(128)}, f32[8,128,1,8]{1,3,2,0:T(8,128)S(1)}, ...), condition=%wide.region_16.17_spmd.clone, body=%wide.region_8.16_spmd.clone.sunk | while | flops 5510830080 | bytes 139387504 | solution.py:160
  225.7 63.4 %conditional.3 = ((f32[8,128,1,8]{1,3,2,0:T(8,128)S(1)}, f32[8,128,1,8]{1,3,2,0:T(8,128)S(1)}, f32[8,128,1,8,128]{4,1,3,2,0:T(8,128)})) conditional(s32[]{:T(128)} %convert_element_type.132, (f32[8,128,1,8]{1,3,2,0:T(8,128)S(1)}, f32[8,128,1,8]{1,3,2,0:T(8,128)S(1)}, f32[8,128,1,8,128]{4,1,3,2,0:T(8,128)}) %tuple.74, (s32[]{:T(128)}, ...), branch_computations={%region_10.10_spmd, %region_11.15_spmd} | conditional | flops 5505423360 | bytes 137950592 | solution.py:158
  226.7 19.1 %fusion.2 = (f32[128,8]{0,1:T(8,128)S(1)}, f32[128,8,10240]{2,0,1:T(8,128)}) fusion(pred[128,10240]{1,0:T(8,128)(4,1)S(1)} %get-tuple-element.251, bf16[128,8,128]{0,2,1:T(8,128)(2,1)S(1)} %bitcast.198, bf16[10240,1,128]{2,0,1:T(8,128)(2,1)} %get-tuple-element.253), kind=kOutput, calls=%fused_computation.7 | convolution fusion | flops 2715810816 | bytes 46141440 | tf_op jit(solution)/shard_map/while/body/eval_jaxpr/cond/branch_1_fun/qkgd,nkd->qkgn/dot_general | solution.py:132
  245.9 19.7 %fusion.4 = f32[128,8]{0,1:T(8,128)S(1)} fusion(f32[128,8,10240]{2,0,1:T(8,128)} %get-tuple-element.390, f32[128,8]{0,1:T(8,128)S(1)} %get-tuple-element.384, pred[128,10240]{1,0:T(8,128)(4,1)S(1)} %get-tuple-element.251), kind=kLoop, calls=%fused_computation.9 | loop fusion | flops 52427776 | bytes 43261952 | tf_op jit(solution)/shard_map/while/body/eval_jaxpr/cond/branch_1_fun/reduce_sum | solution.py:141
  268.7 20.4 %fusion.32 = f32[8,128,1,8,128]{4,1,3,2,0:T(8,128)} fusion(f32[8,128,1,8,128]{4,1,3,2,0:T(8,128)} %get-tuple-element.255, s32[]{:T(128)} %select_n.131, f32[1,128,1,8,128]{4,1,3,2,0:T(8,128)S(1)} %constant_dynamic-slice_fusion, bf16[10240,1,128]{2,0,1:T(8,128)(2,1)} %get-tuple-element.256, f32[128,8,10240]{2,0,1:T(8,128)} %get-tuple-element.390, ...), kind=kOutput, calls=%fused_computation.20 | convolution fusion | flops 2737176576 | bytes 46932992 | tf_op jit(solution)/shard_map/while/body/eval_jaxpr/cond/branch_1_fun/qkgn,nkd->qkgd/dot_general | solution.py:142
  293.6 63.4 %conditional.3 = ((f32[8,128,1,8]{1,3,2,0:T(8,128)S(1)}, f32[8,128,1,8]{1,3,2,0:T(8,128)S(1)}, f32[8,128,1,8,128]{4,1,3,2,0:T(8,128)})) conditional(s32[]{:T(128)} %convert_element_type.132, (f32[8,128,1,8]{1,3,2,0:T(8,128)S(1)}, f32[8,128,1,8]{1,3,2,0:T(8,128)S(1)}, f32[8,128,1,8,128]{4,1,3,2,0:T(8,128)}) %tuple.74, (s32[]{:T(128)}, ...), branch_computations={%region_10.10_spmd, %region_11.15_spmd} | conditional | flops 5505423360 | bytes 137950592 | solution.py:158
  294.6 19.1 %fusion.2 = (f32[128,8]{0,1:T(8,128)S(1)}, f32[128,8,10240]{2,0,1:T(8,128)}) fusion(pred[128,10240]{1,0:T(8,128)(4,1)S(1)} %get-tuple-element.251, bf16[128,8,128]{0,2,1:T(8,128)(2,1)S(1)} %bitcast.198, bf16[10240,1,128]{2,0,1:T(8,128)(2,1)} %get-tuple-element.253), kind=kOutput, calls=%fused_computation.7 | convolution fusion | flops 2715810816 | bytes 46141440 | tf_op jit(solution)/shard_map/while/body/eval_jaxpr/cond/branch_1_fun/qkgd,nkd->qkgn/dot_general | solution.py:132
  313.8 19.7 %fusion.4 = f32[128,8]{0,1:T(8,128)S(1)} fusion(f32[128,8,10240]{2,0,1:T(8,128)} %get-tuple-element.390, f32[128,8]{0,1:T(8,128)S(1)} %get-tuple-element.384, pred[128,10240]{1,0:T(8,128)(4,1)S(1)} %get-tuple-element.251), kind=kLoop, calls=%fused_computation.9 | loop fusion | flops 52427776 | bytes 43261952 | tf_op jit(solution)/shard_map/while/body/eval_jaxpr/cond/branch_1_fun/reduce_sum | solution.py:141
  336.6 20.4 %fusion.32 = f32[8,128,1,8,128]{4,1,3,2,0:T(8,128)} fusion(f32[8,128,1,8,128]{4,1,3,2,0:T(8,128)} %get-tuple-element.255, s32[]{:T(128)} %select_n.131, f32[1,128,1,8,128]{4,1,3,2,0:T(8,128)S(1)} %constant_dynamic-slice_fusion, bf16[10240,1,128]{2,0,1:T(8,128)(2,1)} %get-tuple-element.256, f32[128,8,10240]{2,0,1:T(8,128)} %get-tuple-element.390, ...), kind=kOutput, calls=%fused_computation.20 | convolution fusion | flops 2737176576 | bytes 46932992 | tf_op jit(solution)/shard_map/while/body/eval_jaxpr/cond/branch_1_fun/qkgn,nkd->qkgd/dot_general | solution.py:142
  361.5 63.4 %conditional.3 = ((f32[8,128,1,8]{1,3,2,0:T(8,128)S(1)}, f32[8,128,1,8]{1,3,2,0:T(8,128)S(1)}, f32[8,128,1,8,128]{4,1,3,2,0:T(8,128)})) conditional(s32[]{:T(128)} %convert_element_type.132, (f32[8,128,1,8]{1,3,2,0:T(8,128)S(1)}, f32[8,128,1,8]{1,3,2,0:T(8,128)S(1)}, f32[8,128,1,8,128]{4,1,3,2,0:T(8,128)}) %tuple.74, (s32[]{:T(128)}, ...), branch_computations={%region_10.10_spmd, %region_11.15_spmd} | conditional | flops 5505423360 | bytes 137950592 | solution.py:158
  362.5 19.1 %fusion.2 = (f32[128,8]{0,1:T(8,128)S(1)}, f32[128,8,10240]{2,0,1:T(8,128)}) fusion(pred[128,10240]{1,0:T(8,128)(4,1)S(1)} %get-tuple-element.251, bf16[128,8,128]{0,2,1:T(8,128)(2,1)S(1)} %bitcast.198, bf16[10240,1,128]{2,0,1:T(8,128)(2,1)} %get-tuple-element.253), kind=kOutput, calls=%fused_computation.7 | convolution fusion | flops 2715810816 | bytes 46141440 | tf_op jit(solution)/shard_map/while/body/eval_jaxpr/cond/branch_1_fun/qkgd,nkd->qkgn/dot_general | solution.py:132
  381.7 19.7 %fusion.4 = f32[128,8]{0,1:T(8,128)S(1)} fusion(f32[128,8,10240]{2,0,1:T(8,128)} %get-tuple-element.390, f32[128,8]{0,1:T(8,128)S(1)} %get-tuple-element.384, pred[128,10240]{1,0:T(8,128)(4,1)S(1)} %get-tuple-element.251), kind=kLoop, calls=%fused_computation.9 | loop fusion | flops 52427776 | bytes 43261952 | tf_op jit(solution)/shard_map/while/body/eval_jaxpr/cond/branch_1_fun/reduce_sum | solution.py:141
  404.5 20.4 %fusion.32 = f32[8,128,1,8,128]{4,1,3,2,0:T(8,128)} fusion(f32[8,128,1,8,128]{4,1,3,2,0:T(8,128)} %get-tuple-element.255, s32[]{:T(128)} %select_n.131, f32[1,128,1,8,128]{4,1,3,2,0:T(8,128)S(1)} %constant_dynamic-slice_fusion, bf16[10240,1,128]{2,0,1:T(8,128)(2,1)} %get-tuple-element.256, f32[128,8,10240]{2,0,1:T(8,128)} %get-tuple-element.390, ...), kind=kOutput, calls=%fused_computation.20 | convolution fusion | flops 2737176576 | bytes 46932992 | tf_op jit(solution)/shard_map/while/body/eval_jaxpr/cond/branch_1_fun/qkgn,nkd->qkgd/dot_general | solution.py:142
  429.4 63.4 %conditional.3 = ((f32[8,128,1,8]{1,3,2,0:T(8,128)S(1)}, f32[8,128,1,8]{1,3,2,0:T(8,128)S(1)}, f32[8,128,1,8,128]{4,1,3,2,0:T(8,128)})) conditional(s32[]{:T(128)} %convert_element_type.132, (f32[8,128,1,8]{1,3,2,0:T(8,128)S(1)}, f32[8,128,1,8]{1,3,2,0:T(8,128)S(1)}, f32[8,128,1,8,128]{4,1,3,2,0:T(8,128)}) %tuple.74, (s32[]{:T(128)}, ...), branch_computations={%region_10.10_spmd, %region_11.15_spmd} | conditional | flops 5505423360 | bytes 137950592 | solution.py:158
  430.4 19.1 %fusion.2 = (f32[128,8]{0,1:T(8,128)S(1)}, f32[128,8,10240]{2,0,1:T(8,128)}) fusion(pred[128,10240]{1,0:T(8,128)(4,1)S(1)} %get-tuple-element.251, bf16[128,8,128]{0,2,1:T(8,128)(2,1)S(1)} %bitcast.198, bf16[10240,1,128]{2,0,1:T(8,128)(2,1)} %get-tuple-element.253), kind=kOutput, calls=%fused_computation.7 | convolution fusion | flops 2715810816 | bytes 46141440 | tf_op jit(solution)/shard_map/while/body/eval_jaxpr/cond/branch_1_fun/qkgd,nkd->qkgn/dot_general | solution.py:132
  449.6 19.7 %fusion.4 = f32[128,8]{0,1:T(8,128)S(1)} fusion(f32[128,8,10240]{2,0,1:T(8,128)} %get-tuple-element.390, f32[128,8]{0,1:T(8,128)S(1)} %get-tuple-element.384, pred[128,10240]{1,0:T(8,128)(4,1)S(1)} %get-tuple-element.251), kind=kLoop, calls=%fused_computation.9 | loop fusion | flops 52427776 | bytes 43261952 | tf_op jit(solution)/shard_map/while/body/eval_jaxpr/cond/branch_1_fun/reduce_sum | solution.py:141
  472.4 20.4 %fusion.32 = f32[8,128,1,8,128]{4,1,3,2,0:T(8,128)} fusion(f32[8,128,1,8,128]{4,1,3,2,0:T(8,128)} %get-tuple-element.255, s32[]{:T(128)} %select_n.131, f32[1,128,1,8,128]{4,1,3,2,0:T(8,128)S(1)} %constant_dynamic-slice_fusion, bf16[10240,1,128]{2,0,1:T(8,128)(2,1)} %get-tuple-element.256, f32[128,8,10240]{2,0,1:T(8,128)} %get-tuple-element.390, ...), kind=kOutput, calls=%fused_computation.20 | convolution fusion | flops 2737176576 | bytes 46932992 | tf_op jit(solution)/shard_map/while/body/eval_jaxpr/cond/branch_1_fun/qkgn,nkd->qkgd/dot_general | solution.py:142
  497.3 63.4 %conditional.3 = ((f32[8,128,1,8]{1,3,2,0:T(8,128)S(1)}, f32[8,128,1,8]{1,3,2,0:T(8,128)S(1)}, f32[8,128,1,8,128]{4,1,3,2,0:T(8,128)})) conditional(s32[]{:T(128)} %convert_element_type.132, (f32[8,128,1,8]{1,3,2,0:T(8,128)S(1)}, f32[8,128,1,8]{1,3,2,0:T(8,128)S(1)}, f32[8,128,1,8,128]{4,1,3,2,0:T(8,128)}) %tuple.74, (s32[]{:T(128)}, ...), branch_computations={%region_10.10_spmd, %region_11.15_spmd} | conditional | flops 5505423360 | bytes 137950592 | solution.py:158
  498.3 19.1 %fusion.2 = (f32[128,8]{0,1:T(8,128)S(1)}, f32[128,8,10240]{2,0,1:T(8,128)}) fusion(pred[128,10240]{1,0:T(8,128)(4,1)S(1)} %get-tuple-element.251, bf16[128,8,128]{0,2,1:T(8,128)(2,1)S(1)} %bitcast.198, bf16[10240,1,128]{2,0,1:T(8,128)(2,1)} %get-tuple-element.253), kind=kOutput, calls=%fused_computation.7 | convolution fusion | flops 2715810816 | bytes 46141440 | tf_op jit(solution)/shard_map/while/body/eval_jaxpr/cond/branch_1_fun/qkgd,nkd->qkgn/dot_general | solution.py:132
  517.5 19.7 %fusion.4 = f32[128,8]{0,1:T(8,128)S(1)} fusion(f32[128,8,10240]{2,0,1:T(8,128)} %get-tuple-element.390, f32[128,8]{0,1:T(8,128)S(1)} %get-tuple-element.384, pred[128,10240]{1,0:T(8,128)(4,1)S(1)} %get-tuple-element.251), kind=kLoop, calls=%fused_computation.9 | loop fusion | flops 52427776 | bytes 43261952 | tf_op jit(solution)/shard_map/while/body/eval_jaxpr/cond/branch_1_fun/reduce_sum | solution.py:141
  540.3 20.4 %fusion.32 = f32[8,128,1,8,128]{4,1,3,2,0:T(8,128)} fusion(f32[8,128,1,8,128]{4,1,3,2,0:T(8,128)} %get-tuple-element.255, s32[]{:T(128)} %select_n.131, f32[1,128,1,8,128]{4,1,3,2,0:T(8,128)S(1)} %constant_dynamic-slice_fusion, bf16[10240,1,128]{2,0,1:T(8,128)(2,1)} %get-tuple-element.256, f32[128,8,10240]{2,0,1:T(8,128)} %get-tuple-element.390, ...), kind=kOutput, calls=%fused_computation.20 | convolution fusion | flops 2737176576 | bytes 46932992 | tf_op jit(solution)/shard_map/while/body/eval_jaxpr/cond/branch_1_fun/qkgn,nkd->qkgd/dot_general | solution.py:142
  565.2 63.4 %conditional.3 = ((f32[8,128,1,8]{1,3,2,0:T(8,128)S(1)}, f32[8,128,1,8]{1,3,2,0:T(8,128)S(1)}, f32[8,128,1,8,128]{4,1,3,2,0:T(8,128)})) conditional(s32[]{:T(128)} %convert_element_type.132, (f32[8,128,1,8]{1,3,2,0:T(8,128)S(1)}, f32[8,128,1,8]{1,3,2,0:T(8,128)S(1)}, f32[8,128,1,8,128]{4,1,3,2,0:T(8,128)}) %tuple.74, (s32[]{:T(128)}, ...), branch_computations={%region_10.10_spmd, %region_11.15_spmd} | conditional | flops 5505423360 | bytes 137950592 | solution.py:158
  566.2 19.1 %fusion.2 = (f32[128,8]{0,1:T(8,128)S(1)}, f32[128,8,10240]{2,0,1:T(8,128)}) fusion(pred[128,10240]{1,0:T(8,128)(4,1)S(1)} %get-tuple-element.251, bf16[128,8,128]{0,2,1:T(8,128)(2,1)S(1)} %bitcast.198, bf16[10240,1,128]{2,0,1:T(8,128)(2,1)} %get-tuple-element.253), kind=kOutput, calls=%fused_computation.7 | convolution fusion | flops 2715810816 | bytes 46141440 | tf_op jit(solution)/shard_map/while/body/eval_jaxpr/cond/branch_1_fun/qkgd,nkd->qkgn/dot_general | solution.py:132
  585.4 19.7 %fusion.4 = f32[128,8]{0,1:T(8,128)S(1)} fusion(f32[128,8,10240]{2,0,1:T(8,128)} %get-tuple-element.390, f32[128,8]{0,1:T(8,128)S(1)} %get-tuple-element.384, pred[128,10240]{1,0:T(8,128)(4,1)S(1)} %get-tuple-element.251), kind=kLoop, calls=%fused_computation.9 | loop fusion | flops 52427776 | bytes 43261952 | tf_op jit(solution)/shard_map/while/body/eval_jaxpr/cond/branch_1_fun/reduce_sum | solution.py:141
  608.2 20.4 %fusion.32 = f32[8,128,1,8,128]{4,1,3,2,0:T(8,128)} fusion(f32[8,128,1,8,128]{4,1,3,2,0:T(8,128)} %get-tuple-element.255, s32[]{:T(128)} %select_n.131, f32[1,128,1,8,128]{4,1,3,2,0:T(8,128)S(1)} %constant_dynamic-slice_fusion, bf16[10240,1,128]{2,0,1:T(8,128)(2,1)} %get-tuple-element.256, f32[128,8,10240]{2,0,1:T(8,128)} %get-tuple-element.390, ...), kind=kOutput, calls=%fused_computation.20 | convolution fusion | flops 2737176576 | bytes 46932992 | tf_op jit(solution)/shard_map/while/body/eval_jaxpr/cond/branch_1_fun/qkgn,nkd->qkgd/dot_general | solution.py:142
  633.2 63.4 %conditional.3 = ((f32[8,128,1,8]{1,3,2,0:T(8,128)S(1)}, f32[8,128,1,8]{1,3,2,0:T(8,128)S(1)}, f32[8,128,1,8,128]{4,1,3,2,0:T(8,128)})) conditional(s32[]{:T(128)} %convert_element_type.132, (f32[8,128,1,8]{1,3,2,0:T(8,128)S(1)}, f32[8,128,1,8]{1,3,2,0:T(8,128)S(1)}, f32[8,128,1,8,128]{4,1,3,2,0:T(8,128)}) %tuple.74, (s32[]{:T(128)}, ...), branch_computations={%region_10.10_spmd, %region_11.15_spmd} | conditional | flops 5505423360 | bytes 137950592 | solution.py:158
  634.2 19.1 %fusion.2 = (f32[128,8]{0,1:T(8,128)S(1)}, f32[128,8,10240]{2,0,1:T(8,128)}) fusion(pred[128,10240]{1,0:T(8,128)(4,1)S(1)} %get-tuple-element.251, bf16[128,8,128]{0,2,1:T(8,128)(2,1)S(1)} %bitcast.198, bf16[10240,1,128]{2,0,1:T(8,128)(2,1)} %get-tuple-element.253), kind=kOutput, calls=%fused_computation.7 | convolution fusion | flops 2715810816 | bytes 46141440 | tf_op jit(solution)/shard_map/while/body/eval_jaxpr/cond/branch_1_fun/qkgd,nkd->qkgn/dot_general | solution.py:132
  653.3 19.7 %fusion.4 = f32[128,8]{0,1:T(8,128)S(1)} fusion(f32[128,8,10240]{2,0,1:T(8,128)} %get-tuple-element.390, f32[128,8]{0,1:T(8,128)S(1)} %get-tuple-element.384, pred[128,10240]{1,0:T(8,128)(4,1)S(1)} %get-tuple-element.251), kind=kLoop, calls=%fused_computation.9 | loop fusion | flops 52427776 | bytes 43261952 | tf_op jit(solution)/shard_map/while/body/eval_jaxpr/cond/branch_1_fun/reduce_sum | solution.py:141
  676.1 20.4 %fusion.32 = f32[8,128,1,8,128]{4,1,3,2,0:T(8,128)} fusion(f32[8,128,1,8,128]{4,1,3,2,0:T(8,128)} %get-tuple-element.255, s32[]{:T(128)} %select_n.131, f32[1,128,1,8,128]{4,1,3,2,0:T(8,128)S(1)} %constant_dynamic-slice_fusion, bf16[10240,1,128]{2,0,1:T(8,128)(2,1)} %get-tuple-element.256, f32[128,8,10240]{2,0,1:T(8,128)} %get-tuple-element.390, ...), kind=kOutput, calls=%fused_computation.20 | convolution fusion | flops 2737176576 | bytes 46932992 | tf_op jit(solution)/shard_map/while/body/eval_jaxpr/cond/branch_1_fun/qkgn,nkd->qkgd/dot_general | solution.py:142
  701.1 63.4 %conditional.3 = ((f32[8,128,1,8]{1,3,2,0:T(8,128)S(1)}, f32[8,128,1,8]{1,3,2,0:T(8,128)S(1)}, f32[8,128,1,8,128]{4,1,3,2,0:T(8,128)})) conditional(s32[]{:T(128)} %convert_element_type.132, (f32[8,128,1,8]{1,3,2,0:T(8,128)S(1)}, f32[8,128,1,8]{1,3,2,0:T(8,128)S(1)}, f32[8,128,1,8,128]{4,1,3,2,0:T(8,128)}) %tuple.74, (s32[]{:T(128)}, ...), branch_computations={%region_10.10_spmd, %region_11.15_spmd} | conditional | flops 5505423360 | bytes 137950592 | solution.py:158
  702.1 19.1 %fusion.2 = (f32[128,8]{0,1:T(8,128)S(1)}, f32[128,8,10240]{2,0,1:T(8,128)}) fusion(pred[128,10240]{1,0:T(8,128)(4,1)S(1)} %get-tuple-element.251, bf16[128,8,128]{0,2,1:T(8,128)(2,1)S(1)} %bitcast.198, bf16[10240,1,128]{2,0,1:T(8,128)(2,1)} %get-tuple-element.253), kind=kOutput, calls=%fused_computation.7 | convolution fusion | flops 2715810816 | bytes 46141440 | tf_op jit(solution)/shard_map/while/body/eval_jaxpr/cond/branch_1_fun/qkgd,nkd->qkgn/dot_general | solution.py:132
  721.2 19.7 %fusion.4 = f32[128,8]{0,1:T(8,128)S(1)} fusion(f32[128,8,10240]{2,0,1:T(8,128)} %get-tuple-element.390, f32[128,8]{0,1:T(8,128)S(1)} %get-tuple-element.384, pred[128,10240]{1,0:T(8,128)(4,1)S(1)} %get-tuple-element.251), kind=kLoop, calls=%fused_computation.9 | loop fusion | flops 52427776 | bytes 43261952 | tf_op jit(solution)/shard_map/while/body/eval_jaxpr/cond/branch_1_fun/reduce_sum | solution.py:141
  744.1 20.4 %fusion.32 = f32[8,128,1,8,128]{4,1,3,2,0:T(8,128)} fusion(f32[8,128,1,8,128]{4,1,3,2,0:T(8,128)} %get-tuple-element.255, s32[]{:T(128)} %select_n.131, f32[1,128,1,8,128]{4,1,3,2,0:T(8,128)S(1)} %constant_dynamic-slice_fusion, bf16[10240,1,128]{2,0,1:T(8,128)(2,1)} %get-tuple-element.256, f32[128,8,10240]{2,0,1:T(8,128)} %get-tuple-element.390, ...), kind=kOutput, calls=%fused_computation.20 | convolution fusion | flops 2737176576 | bytes 46932992 | tf_op jit(solution)/shard_map/while/body/eval_jaxpr/cond/branch_1_fun/qkgn,nkd->qkgd/dot_general | solution.py:142
  764.5 5.3 copy.52
  772.6 17.4 %convolution_convert_fusion = bf16[8,128,4,1280]{3,1,2,0:T(8,128)(2,1)} fusion(bf16[8,128,1024,1]{1,2,3,0:T(8,128)(2,1)S(1)} %bitcast.202, bf16[1024,4,1280]{2,1,0:T(4,128)(2,1)} %reshape_squeeze.11), kind=kOutput, calls=%fused_computation.54 | convolution fusion | flops 10742661120 | bytes 23068672 | tf_op jit(solution)/shard_map/dpqe,etf->dtpqf/dot_general | solution.py:171
  790.1 4.9 all-to-all-start.1
  795.1 141.1 %all-to-all-done.1 = bf16[32,128,1280]{2,1,0:T(8,128)(2,1)} async-done(((bf16[32,128,1280]{2,1,0:T(8,128)(2,1)}), bf16[32,128,1280]{2,1,0:T(8,128)(2,1)}, u32[]{:S(2)}, u32[]{:S(2)}) %all-to-all-start.1) | async-done | bytes 10485792 | tf_op jit(solution)/shard_map/all_to_all | solution.py:175
  936.3 8.5 convert_reduce_fusion
  944.8 4.2 gather_fusion.3
  954.4 14.7 %collective-permute-done = bf16[1,256,1280]{2,1,0:T(8,128)(2,1)S(1)} collective-permute-done((bf16[1,256,1280]{2,1,0:T(8,128)(2,1)}, bf16[1,256,1280]{2,1,0:T(8,128)(2,1)S(1)}, u32[]{:S(2)}, u32[]{:S(2)}) %collective-permute-start) | collective-permute-done | bytes 655392 | tf_op jit(solution)/shard_map/ppermute | solution.py:17
  (207 shorter events, 86.2 us)
Async XLA Ops:
  7.2 42.6 %copy-start = (bf16[1,5120,256]{2,1,0:T(8,128)(2,1)S(1)}, bf16[1,5120,256]{2,1,0:T(8,128)(2,1)}, u32[]{:S(2)}) copy-start(bf16[1,5120,256]{2,1,0:T(8,128)(2,1)} %param.22) | copy-start | bytes 7864324
  7.2 40.2 %all-gather.6.cloned.1.call-start = ((), (), s32[]{:S(2)}) async-start(), calls=%async_computation.3 | async-start | bytes 3276800 | tf_op jit(solution)/shard_map/all_gather | solution.py:62
  7.9 206.6 %all-gather.4.cloned.1.call-start = ((), (), s32[]{:S(2)}) async-start(), calls=%async_computation.2 | async-start | bytes 5898240 | tf_op jit(solution)/shard_map/all_gather | solution.py:110
  8.7 43.7 %copy-start.5 = (bf16[1,1024,1,256]{3,1,2,0:T(8,128)(2,1)S(1)}, bf16[1,1024,1,256]{3,1,2,0:T(8,128)(2,1)}, u32[]{:S(2)}) copy-start(bf16[1,1024,1,256]{3,1,2,0:T(8,128)(2,1)} %param.24) | copy-start | bytes 1572868
  49.8 4.2 copy-start.15
  49.8 5.3 copy-start.11
  55.2 17.0 %copy-start.7 = (s32[4,1]{0,1:T(1,128)}, s32[4,1]{0,1:T(1,128)S(1)}, u32[]{:S(2)}) copy-start(s32[4,1]{0,1:T(1,128)S(1)} %reduce-window.13) | copy-start | bytes 52
  55.4 8.3 copy-start.9
  67.4 144.7 %all-to-all-start = ((bf16[8,128,1024]{2,1,0:T(8,128)(2,1)}), bf16[8,128,1024]{2,1,0:T(8,128)(2,1)S(1)}, u32[]{:S(2)}, u32[]{:S(2)}) async-start(bf16[8,128,1024]{2,1,0:T(8,128)(2,1)} %copy.50), calls=%async_computation | async-start | bytes 4194304 | tf_op jit(solution)/shard_map/all_to_all | solution.py:89
  72.3 63.0 %copy-start.2 = (s32[2048]{0:T(1024)}, s32[2048]{0:T(1024)S(1)}, u32[]{:S(2)}) copy-start(s32[2048]{0:T(1024)S(1)} %convert_reduce_fusion.2) | copy-start | bytes 24580
  78.5 56.8 %copy-start.13 = (s32[1,4]{1,0:T(1,128)S(1)}, s32[1,4]{1,0:T(1,128)}, u32[]{:S(2)}) copy-start(s32[1,4]{1,0:T(1,128)} %param.25) | copy-start | bytes 52
  245.9 19.7 %copy-start.6 = (s32[4]{0:T(128)S(1)}, s32[4]{0:T(128)}, u32[]{:S(2)}) copy-start(s32[4]{0:T(128)} %constant.191.clone) | copy-start | bytes 52 | tf_op jit(solution)/shard_map/while/body/eval_jaxpr/cond
  245.9 22.2 %copy-start.17 = (s32[5]{0:T(128)S(1)}, s32[5]{0:T(128)}, u32[]{:S(2)}) copy-start(s32[5]{0:T(128)} %constant.197.clone) | copy-start | bytes 64 | tf_op jit(solution)/shard_map/while/body/eval_jaxpr/cond
  313.8 19.7 %copy-start.6 = (s32[4]{0:T(128)S(1)}, s32[4]{0:T(128)}, u32[]{:S(2)}) copy-start(s32[4]{0:T(128)} %constant.191.clone) | copy-start | bytes 52 | tf_op jit(solution)/shard_map/while/body/eval_jaxpr/cond
  313.8 22.2 %copy-start.17 = (s32[5]{0:T(128)S(1)}, s32[5]{0:T(128)}, u32[]{:S(2)}) copy-start(s32[5]{0:T(128)} %constant.197.clone) | copy-start | bytes 64 | tf_op jit(solution)/shard_map/while/body/eval_jaxpr/cond
  381.7 19.7 %copy-start.6 = (s32[4]{0:T(128)S(1)}, s32[4]{0:T(128)}, u32[]{:S(2)}) copy-start(s32[4]{0:T(128)} %constant.191.clone) | copy-start | bytes 52 | tf_op jit(solution)/shard_map/while/body/eval_jaxpr/cond
  381.7 22.2 %copy-start.17 = (s32[5]{0:T(128)S(1)}, s32[5]{0:T(128)}, u32[]{:S(2)}) copy-start(s32[5]{0:T(128)} %constant.197.clone) | copy-start | bytes 64 | tf_op jit(solution)/shard_map/while/body/eval_jaxpr/cond
  449.6 19.7 %copy-start.6 = (s32[4]{0:T(128)S(1)}, s32[4]{0:T(128)}, u32[]{:S(2)}) copy-start(s32[4]{0:T(128)} %constant.191.clone) | copy-start | bytes 52 | tf_op jit(solution)/shard_map/while/body/eval_jaxpr/cond
  449.6 22.2 %copy-start.17 = (s32[5]{0:T(128)S(1)}, s32[5]{0:T(128)}, u32[]{:S(2)}) copy-start(s32[5]{0:T(128)} %constant.197.clone) | copy-start | bytes 64 | tf_op jit(solution)/shard_map/while/body/eval_jaxpr/cond
  517.5 19.7 %copy-start.6 = (s32[4]{0:T(128)S(1)}, s32[4]{0:T(128)}, u32[]{:S(2)}) copy-start(s32[4]{0:T(128)} %constant.191.clone) | copy-start | bytes 52 | tf_op jit(solution)/shard_map/while/body/eval_jaxpr/cond
  517.5 22.2 %copy-start.17 = (s32[5]{0:T(128)S(1)}, s32[5]{0:T(128)}, u32[]{:S(2)}) copy-start(s32[5]{0:T(128)} %constant.197.clone) | copy-start | bytes 64 | tf_op jit(solution)/shard_map/while/body/eval_jaxpr/cond
  585.4 19.7 %copy-start.6 = (s32[4]{0:T(128)S(1)}, s32[4]{0:T(128)}, u32[]{:S(2)}) copy-start(s32[4]{0:T(128)} %constant.191.clone) | copy-start | bytes 52 | tf_op jit(solution)/shard_map/while/body/eval_jaxpr/cond
  585.4 22.2 %copy-start.17 = (s32[5]{0:T(128)S(1)}, s32[5]{0:T(128)}, u32[]{:S(2)}) copy-start(s32[5]{0:T(128)} %constant.197.clone) | copy-start | bytes 64 | tf_op jit(solution)/shard_map/while/body/eval_jaxpr/cond
  653.3 19.7 %copy-start.6 = (s32[4]{0:T(128)S(1)}, s32[4]{0:T(128)}, u32[]{:S(2)}) copy-start(s32[4]{0:T(128)} %constant.191.clone) | copy-start | bytes 52 | tf_op jit(solution)/shard_map/while/body/eval_jaxpr/cond
  653.3 22.2 %copy-start.17 = (s32[5]{0:T(128)S(1)}, s32[5]{0:T(128)}, u32[]{:S(2)}) copy-start(s32[5]{0:T(128)} %constant.197.clone) | copy-start | bytes 64 | tf_op jit(solution)/shard_map/while/body/eval_jaxpr/cond
  721.2 19.7 %copy-start.6 = (s32[4]{0:T(128)S(1)}, s32[4]{0:T(128)}, u32[]{:S(2)}) copy-start(s32[4]{0:T(128)} %constant.191.clone) | copy-start | bytes 52 | tf_op jit(solution)/shard_map/while/body/eval_jaxpr/cond
  721.2 22.2 %copy-start.17 = (s32[5]{0:T(128)S(1)}, s32[5]{0:T(128)}, u32[]{:S(2)}) copy-start(s32[5]{0:T(128)} %constant.197.clone) | copy-start | bytes 64 | tf_op jit(solution)/shard_map/while/body/eval_jaxpr/cond
  790.1 4.9 copy-start.10
  790.1 146.2 %all-to-all-start.1 = ((bf16[32,128,1280]{2,1,0:T(8,128)(2,1)}), bf16[32,128,1280]{2,1,0:T(8,128)(2,1)}, u32[]{:S(2)}, u32[]{:S(2)}) async-start(bf16[32,128,1280]{2,1,0:T(8,128)(2,1)} %bitcast.199), calls=%async_computation.1 | async-start | bytes 20971520 | tf_op jit(solution)/shard_map/all_to_all | solution.py:175
  795.1 153.9 %copy-start.4 = (bf16[1,256,1280]{2,1,0:T(8,128)(2,1)S(1)}, bf16[1,256,1280]{2,1,0:T(8,128)(2,1)}, u32[]{:S(2)}) copy-start(bf16[1,256,1280]{2,1,0:T(8,128)(2,1)} %param.19) | copy-start | bytes 1966084
  936.3 33.7 %copy-start.1 = (bf16[1,5120,256]{2,1,0:T(8,128)(2,1)S(1)}, bf16[1,5120,256]{2,1,0:T(8,128)(2,1)}, u32[]{:S(2)}) copy-start(bf16[1,5120,256]{2,1,0:T(8,128)(2,1)} %param.22) | copy-start | bytes 7864324
  944.8 8.1 copy-start.8
  944.8 8.1 copy-start.12
  944.8 8.1 copy-start.14
  944.8 8.1 copy-start.3
  944.8 8.3 copy-start.16
  951.4 17.7 %collective-permute-start = (bf16[1,256,1280]{2,1,0:T(8,128)(2,1)}, bf16[1,256,1280]{2,1,0:T(8,128)(2,1)S(1)}, u32[]{:S(2)}, u32[]{:S(2)}) collective-permute-start(bf16[1,256,1280]{2,1,0:T(8,128)(2,1)} %fusion.61), channel_id=1, source_target_pairs={{96,0},{0,32},{32,64},{64,96},{97,1},{1,33},{33,65},{65,97},{98,2}... | collective-permute-start | bytes 1966088 | tf_op jit(solution)/shard_map/ppermute | solution.py:17
Sparse Core Ops, SparseCore 0:
  9.7 37.6 all-gather.5
  53.5 54.2 all-gather.3
where the time goes:
time: 989 us; the launch traced here: 978 us
  matrix products  346 us (35%)
  other arithmetic  214 us (22%)
  waiting for transfers between devices  195 us (20%)
  local copies, waits for them, and re-layouts  185 us (19%)
  between operations  16.1 us (2%)
  starting transfers between devices  11.3 us (1%)
  loops' own time  10.6 us (1%)
    dot_general x8, matrix products, update(): jnp.einsum('qkgn,nkd->qkgd', weights.astype(jnp.bfloat16), value_part, pr...  163 us
    reduce_sum x8, other arithmetic, update(): summed = old_sum[slot_index] * rescale + jnp.sum(weights, axis=3)  158 us
    dot_general x8, matrix products, update(): jnp.einsum('qkgd,nkd->qkgn', query_slot, key_part, preferred_element_type...  153 us
    all_to_all x1, waiting for transfers between devices, on_device(): lax.all_to_all(flat_parts, ('dp', 'tensor'), split_axis=0, concat_axis=0,...  141 us
    gather x1, local copies, waits for them, and re-layouts, on_device(): jnp.take(row_doc, row_index)  56.8 us
    gather x1, local copies, waits for them, and re-layouts, on_device(): jnp.take(cache_doc, cache_index)  56.8 us
    all_gather x1, waiting for transfers between devices, on_device(): full_rows = lax.all_gather(own_rows, 'tensor', axis=1, tiled=True)  38.7 us
    reduce_or x8, other arithmetic, per_slot(): jnp.any(visible)  20.4 us
  transfers between devices with their start and end apart: 5, of which 3 were waited for; matrix products, arithmetic and copies ran while one was open for 16% of the time, Pallas kernels for 0%

commit v1 on v0

v1 whole, which is shorter than its diff:
```python
import functools

import jax
import jax.numpy as jnp
from jax import lax
from jax.experimental import pallas as pl
from jax.experimental.pallas import tpu as pltpu
from jax.sharding import PartitionSpec as P

HEAD = 128
BLOCK = 128
EPS = 1e-06
NEG = -1e30
LOG2E = 1.4426950408889634
MESH = pl.DeviceIdType.MESH
F32 = jnp.float32
BF16 = jnp.bfloat16


def remote(src, dst, sems, index, target):
    return pltpu.make_async_remote_copy(
        src_ref=src,
        dst_ref=dst,
        send_sem=sems[0].at[index],
        recv_sem=sems[1].at[index],
        device_id=target,
        device_id_type=MESH,
    )


def project_kernel(
    n_dp, n_t, tok, gain, wq_hbm, wkv_hbm, cache, q_out, kv_full, cache_full,
    xs, wq, wkv, normed, kv_own, w_sem, loc_sem,
    z_send, z_recv, y_send, y_recv, k_send, k_recv,
):
    rank = lax.axis_index("dp")
    t = lax.axis_index("tensor")
    right, left = lax.rem(t + 1, n_t), lax.rem(t + n_t - 1, n_t)
    over = lax.rem(t + 2, n_t)
    up, down = lax.rem(rank + 2, n_dp), lax.rem(rank + n_dp - 2, n_dp)
    across = lax.rem(rank + 4, n_dp)
    twin = rank + 1 - 2 * lax.rem(rank, 2)
    z, y, k = (z_send, z_recv), (y_send, y_recv), (k_send, k_recv)
    half = BLOCK // 2
    span = cache.shape[0]
    mid = span // 2

    w_copies = [
        pltpu.make_async_copy(wq_hbm, wq, w_sem.at[0]),
        pltpu.make_async_copy(wkv_hbm, wkv, w_sem.at[1]),
    ]

    barrier = pltpu.get_barrier_semaphore()
    for other in (left, right):
        pl.semaphore_signal(barrier, inc=1, device_id={"tensor": other}, device_id_type=MESH)
    for step in range(1, n_dp):
        other = lax.rem(rank + step, n_dp)
        pl.semaphore_signal(barrier, inc=1, device_id={"dp": other}, device_id_type=MESH)
    pl.semaphore_wait(barrier, 2 + n_dp - 1)

    def rows(block, lower, upper):
        return pl.ds(block * BLOCK + lower, upper - lower)

    def z_own(block, way, target):
        part = rows(block, 0, BLOCK)
        return remote(tok.at[part], xs.at[t, part], z, block * 4 + way, {"tensor": target})

    def z_own_in(block, way, source):
        part = xs.at[source, rows(block, 0, BLOCK)]
        return remote(part, part, z, block * 4 + way, {"tensor": source})

    def z_far(block, way, slot, target):
        low = 0 if way == 0 else half
        part = xs.at[slot, rows(block, low, low + half)]
        return remote(part, part, z, block * 4 + 2 + way, {"tensor": target})

    started = []

    def go(copy):
        copy.start()
        started.append(copy)

    go(z_own(0, 0, right))
    go(z_own(0, 1, left))
    go(remote(cache, cache_full.at[rank], y, 0, {"dp": up}))
    go(remote(cache, cache_full.at[rank], y, 1, {"dp": down}))
    go(remote(cache, cache_full.at[rank], y, 4, {"dp": twin}))
    own_cache = pltpu.make_async_copy(cache, cache_full.at[rank], loc_sem.at[0])
    own_cache.start()
    for copy in w_copies:
        copy.start()
    xs[t] = tok[...]

    def y_in(index, slot, lower, upper):
        part = cache_full.at[slot, pl.ds(lower, upper - lower)]
        return remote(part, part, y, index, {"dp": twin})

    def y_out(index, slot, lower, upper, target):
        part = cache_full.at[slot, pl.ds(lower, upper - lower)]
        go(remote(part, part, y, index, {"dp": target}))

    def forward_z(block):
        z_own_in(block, 0, left).wait_recv()
        go(z_far(block, 0, left, right))
        z_own_in(block, 1, right).wait_recv()
        go(z_far(block, 1, right, left))

    def far_z(block):
        z_far(block, 0, over, right).wait_recv()
        z_far(block, 1, over, left).wait_recv()

    def compute(block):
        def norm_rows(step, carry):
            low = pl.multiple_of(block * BLOCK + step * 16, 16)
            low_here = pl.multiple_of(step * 16, 16)
            parts = [xs[i, pl.ds(low, 16), :].astype(F32) for i in range(n_t)]
            total = jnp.sum(parts[0] * parts[0], axis=1, keepdims=True)
            for part in parts[1:]:
                total += jnp.sum(part * part, axis=1, keepdims=True)
            width = parts[0].shape[1]
            factor = lax.rsqrt(total / (width * n_t) + EPS)
            for i, part in enumerate(parts):
                cols = pl.ds(i * width, width)
                scaled = part * factor * gain[:, cols].astype(F32)
                normed[pl.ds(low_here, 16), cols] = scaled.astype(BF16)
            return carry

        lax.fori_loop(0, BLOCK // 16, norm_rows, 0)

        if block == 0:
            w_copies[1].wait()
        made = jnp.dot(normed[...], wkv[...], preferred_element_type=F32)
        kv_own[pl.ds(block * BLOCK, BLOCK), :] = made.astype(BF16)
        part = pl.ds(block * BLOCK, BLOCK)
        for step in range(1, n_dp):
            other = lax.rem(rank + step, n_dp)
            index = block * (n_dp - 1) + step - 1
            go(remote(kv_own.at[part], kv_full.at[rank, part], k, index, {"dp": other}))
        if block == 0:
            w_copies[0].wait()

        def query_tile(n, carry):
            cols = pl.ds(pl.multiple_of(n * 256, 256), 256)
            tile = jnp.dot(normed[...], wq[:, cols], preferred_element_type=F32).astype(BF16)
            q_out[block, 2 * n] = tile[:, :HEAD]
            q_out[block, 2 * n + 1] = tile[:, HEAD:]
            return carry

        lax.fori_loop(0, wq.shape[1] // 256, query_tile, 0)

    forward_z(0)
    go(z_own(1, 0, right))
    go(z_own(1, 1, left))
    far_z(0)
    y_in(0, down, 0, span).wait_recv()
    y_out(2, down, 0, mid, up)
    y_out(5, down, 0, span, twin)
    y_in(1, up, 0, span).wait_recv()
    y_out(3, up, mid, span, down)
    y_out(6, up, 0, span, twin)
    compute(0)
    forward_z(1)
    y_in(2, across, 0, mid).wait_recv()
    y_out(7, across, 0, mid, twin)
    y_in(3, across, mid, span).wait_recv()
    y_out(8, across, mid, span, twin)
    far_z(1)
    compute(1)

    own_kv = pltpu.make_async_copy(kv_own, kv_full.at[rank], loc_sem.at[1])
    own_kv.start()
    twin_of = lambda r: r + 1 - 2 * lax.rem(r, 2)
    y_in(4, twin, 0, span).wait_recv()
    y_in(5, twin_of(down), 0, span).wait_recv()
    y_in(6, twin_of(up), 0, span).wait_recv()
    y_in(7, twin_of(across), 0, mid).wait_recv()
    y_in(8, twin_of(across), mid, span).wait_recv()
    for block in range(2):
        part = pl.ds(block * BLOCK, BLOCK)
        for step in range(1, n_dp):
            source = lax.rem(rank + n_dp - step, n_dp)
            index = block * (n_dp - 1) + step - 1
            here = kv_full.at[source, part]
            remote(here, here, k, index, {"dp": source}).wait_recv()
    own_cache.wait()
    own_kv.wait()
    for copy in started:
        copy.wait_send()


def project(own_rows, gain, w_query, w_kv, cache, n_dp, n_t):
    rows, width = own_rows.shape
    blocks = rows // BLOCK
    full, heads_width = w_query.shape
    kv_width = w_kv.shape[1]
    heads = heads_width // HEAD
    span = cache.shape[0]
    vmem = pl.BlockSpec(memory_space=pltpu.VMEM)
    anywhere = pl.BlockSpec(memory_space=pl.ANY)
    return pl.pallas_call(
        functools.partial(project_kernel, n_dp, n_t),
        out_shape=(
            jax.ShapeDtypeStruct((blocks, heads, BLOCK, HEAD), BF16),
            jax.ShapeDtypeStruct((n_dp, rows, kv_width), BF16),
            jax.ShapeDtypeStruct((n_dp, span, kv_width), BF16),
        ),
        in_specs=[vmem, vmem, anywhere, anywhere, anywhere],
        out_specs=(vmem, anywhere, anywhere),
        scratch_shapes=[
            pltpu.VMEM((n_t, rows, width), BF16),
            pltpu.VMEM((full, heads_width), BF16),
            pltpu.VMEM((full, kv_width), BF16),
            pltpu.VMEM((BLOCK, full), BF16),
            pltpu.VMEM((rows, kv_width), BF16),
            pltpu.SemaphoreType.DMA((2,)),
            pltpu.SemaphoreType.DMA((2,)),
            pltpu.SemaphoreType.DMA((8,)),
            pltpu.SemaphoreType.DMA((8,)),
            pltpu.SemaphoreType.DMA((9,)),
            pltpu.SemaphoreType.DMA((9,)),
            pltpu.SemaphoreType.DMA((2 * (n_dp - 1),)),
            pltpu.SemaphoreType.DMA((2 * (n_dp - 1),)),
        ],
        compiler_params=pltpu.CompilerParams(
            collective_id=0, has_side_effects=True, vmem_limit_bytes=40 * 1024 * 1024
        ),
        name="project",
    )(own_rows, gain, w_query, w_kv, cache)


CHUNK = 512


def attend_kernel(
    n_docs, cache_len, row_len, owner, q, cache, kv, out, held, m_s, l_s, acc_s
):
    rank = lax.axis_index("dp")
    heads = q.shape[1]
    blocks = q.shape[0]
    lanes = heads * BLOCK
    c_len = [cache_len[0, d] for d in range(n_docs)]
    r_len = [row_len[0, d] for d in range(n_docs)]
    r_end, c_end = [], []
    r_sum = c_sum = jnp.int32(0)
    for d in range(n_docs):
        r_sum = r_sum + r_len[d]
        c_sum = c_sum + c_len[d]
        r_end.append(r_sum)
        c_end.append(c_sum)
    r_start = [r_end[d] - r_len[d] for d in range(n_docs)]
    scale = HEAD ** (-0.5) * LOG2E

    def add_where(tests, values):
        total = jnp.where(tests[0], values[0], 0)
        for test, value in zip(tests[1:], values[1:]):
            total = total + jnp.where(test, value, 0)
        return total

    for block in range(blocks):
        first = (rank * blocks + block) * BLOCK
        last = first + BLOCK - 1
        before_first = [r_end[d] <= first for d in range(n_docs)]
        begun = [r_start[d] <= last for d in range(n_docs)]
        c_low = add_where(before_first, c_len)
        c_high = add_where(begun, c_len)
        r_low = add_where(before_first, r_len)
        ended = [r_end[d] <= last for d in range(n_docs)]
        ones = [jnp.int32(1)] * n_docs
        single = add_where(before_first, ones) == add_where(ended, ones)

        row = first + lax.broadcasted_iota(jnp.int32, (1, BLOCK), 1)
        passed = [r_end[d] <= row for d in range(n_docs)]
        reached = [r_start[d] <= row for d in range(n_docs)]
        row_c_low = add_where(passed, c_len)
        row_c_high = add_where(reached, c_len)
        row_r_low = add_where(passed, r_len)

        m_s[...] = jnp.full(m_s.shape, NEG, F32)
        l_s[...] = jnp.zeros(l_s.shape, F32)
        acc_s[...] = jnp.zeros(acc_s.shape, F32)

        def chunk_step(source, start, low_row, high_row, masked):
            keys = source[pl.ds(start, CHUNK), :HEAD]
            values = source[pl.ds(start, CHUNK), HEAD:]
            values_t = values.T
            if masked:
                place = start + lax.broadcasted_iota(jnp.int32, (CHUNK, BLOCK), 0)
                seen = (place >= low_row) & (place < high_row)
            for h in range(0, heads, 2):
                queries = q[block, h : h + 2].reshape(2 * BLOCK, HEAD)
                scores = lax.dot_general(
                    keys, queries, (((1,), (1,)), ((), ())), preferred_element_type=F32
                )
                cols = pl.ds(h * BLOCK, 2 * BLOCK)
                if masked:
                    seen2 = jnp.concatenate([seen, seen], axis=1)
                    scores = jnp.where(seen2, scores, NEG)
                prior = m_s[:, cols]
                newest = jnp.maximum(prior, jnp.max(scores, axis=0, keepdims=True))
                weights = jnp.exp2((scores - newest) * scale)
                if masked:
                    weights = jnp.where(seen2, weights, 0.0)
                rescale = jnp.exp2((prior - newest) * scale)
                m_s[:, cols] = newest
                l_s[:, cols] = l_s[:, cols] * rescale + jnp.sum(weights, axis=0, keepdims=True)
                product = jnp.dot(
                    values_t, weights.astype(BF16), preferred_element_type=F32
                )
                acc_s[:, cols] = acc_s[:, cols] * rescale + product

        def loop_over(source, low, high, low_row, high_row, full_high):
            def one(c, carry):
                start = pl.multiple_of(c * CHUNK, CHUNK)
                whole = single & (start >= low) & (start + CHUNK <= full_high)

                @pl.when(whole)
                def _():
                    chunk_step(source, start, low_row, high_row, False)

                @pl.when(jnp.logical_not(whole))
                def _():
                    chunk_step(source, start, low_row, high_row, True)

                return carry

            lax.fori_loop(low // CHUNK, (high + CHUNK - 1) // CHUNK, one, 0)

        loop_over(cache, c_low, c_high, row_c_low, row_c_high, c_high)
        loop_over(kv, r_low, last + 1, row_r_low, row + 1, first + 1)

        for h in range(heads):
            cols = pl.ds(h * BLOCK, BLOCK)
            done = acc_s[:, cols] / l_s[:, cols]
            out[pl.ds(block * BLOCK, BLOCK), cols] = done.T.astype(BF16)

    def load_of(b, total):
        low = b * BLOCK
        work = low * BLOCK + (BLOCK * (BLOCK - 1)) // 2
        for d in range(n_docs):
            inside = jnp.minimum(r_end[d], low + BLOCK) - jnp.maximum(r_start[d], low)
            work = work + jnp.maximum(inside, 0) * (c_len[d] - r_start[d] + 1)
        return total + jnp.where(owner[b] == rank, work, 0)

    total = lax.fori_loop(0, owner.shape[0], load_of, jnp.int32(0))
    divisor = BLOCK * (cache.shape[0] // 2 + kv.shape[0] // 2)
    held[0, 0] = total.astype(F32) * (1.0 / divisor)


def attend(cache_len, row_len, owner, q, cache, kv):
    blocks, heads = q.shape[:2]
    vmem = pl.BlockSpec(memory_space=pltpu.VMEM)
    smem = pl.BlockSpec(memory_space=pltpu.SMEM)
    return pl.pallas_call(
        functools.partial(attend_kernel, cache_len.shape[1]),
        out_shape=(
            jax.ShapeDtypeStruct((blocks * BLOCK, heads * HEAD), BF16),
            jax.ShapeDtypeStruct((1, 1), F32),
        ),
        in_specs=[smem, smem, smem, vmem, vmem, vmem],
        out_specs=(vmem, smem),
        scratch_shapes=[
            pltpu.VMEM((1, heads * BLOCK), F32),
            pltpu.VMEM((1, heads * BLOCK), F32),
            pltpu.VMEM((HEAD, heads * BLOCK), F32),
        ],
        compiler_params=pltpu.CompilerParams(vmem_limit_bytes=40 * 1024 * 1024),
        name="attend",
    )(cache_len, row_len, owner, q, cache, kv)


PIECES = 4


def output_kernel(
    n_pipe, n_t, att, tok, wo_hbm, out,
    wo, far, far_in, to_right, to_left, own, sent, from_left, from_right, section,
    w_sem, z_send, z_recv, x_send, x_recv,
):
    s = lax.axis_index("pipe")
    t = lax.axis_index("tensor")
    right, left = lax.rem(t + 1, n_t), lax.rem(t + n_t - 1, n_t)
    over = lax.rem(t + 2, n_t)
    ahead, behind = lax.rem(s + 1, n_pipe), lax.rem(s + n_pipe - 1, n_pipe)
    z, x = (z_send, z_recv), (x_send, x_recv)
    width = tok.shape[1]
    size = tok.shape[0] // PIECES
    half = size // 2
    order = (over, right, left, t)
    w_copies = []
    for i, target in enumerate(order):
        cols = pl.ds(pl.multiple_of(target * width, width), width)
        copy = pltpu.make_async_copy(wo_hbm.at[:, cols], wo.at[i], w_sem.at[i])
        copy.start()
        w_copies.append(copy)

    barrier = pltpu.get_barrier_semaphore()
    for other in (left, right):
        pl.semaphore_signal(barrier, inc=1, device_id={"tensor": other}, device_id_type=MESH)
    for other in (ahead, behind):
        pl.semaphore_signal(barrier, inc=1, device_id={"pipe": other}, device_id_type=MESH)
    pl.semaphore_wait(barrier, 4)

    def multiply(i, store):
        w_copies[i].wait()

        def tile(n, carry):
            cols = pl.ds(pl.multiple_of(n * 256, 256), 256)
            store(cols, jnp.dot(att[...], wo[i, :, cols], preferred_element_type=F32))
            return carry

        lax.fori_loop(0, width // 256, tile, 0)

    started = []

    def go(copy):
        copy.start()
        started.append(copy)

    def span(p, way):
        return pl.ds(p * size + way * half, half)

    def far_copy(p, way):
        target = right if way == 0 else left
        return remote(far.at[span(p, way)], far_in.at[span(p, way)], z, p * 6 + way, {"tensor": target})

    def near_copy(p, way, kind):
        part = span(p, way if kind == 1 else 1 - way)
        target, box = (right, from_left) if way == 0 else (left, from_right)
        return remote(sent.at[way, part], box.at[part], z, p * 6 + 2 + 2 * kind + way, {"tensor": target})

    def store_far(cols, value):
        far[:, cols] = value.astype(BF16)

    multiply(0, store_far)
    for p in range(PIECES):
        for way in range(2):
            go(far_copy(p, way))

    def store_right(cols, value):
        to_right[:, cols] = value

    def store_left(cols, value):
        to_left[:, cols] = value

    multiply(1, store_right)
    multiply(2, store_left)
    held = (to_right, to_left)
    for p in range(PIECES):
        for way in range(2):
            part = span(p, 1 - way)
            sent[way, part, :] = held[way][part, :].astype(BF16)
            go(near_copy(p, way, 0))
        for way in range(2):
            part = span(p, way)
            far_copy(p, way).wait_recv()
            sent[way, part, :] = (held[way][part, :] + far_in[part, :].astype(F32)).astype(BF16)
            go(near_copy(p, way, 1))

    def store_own(cols, value):
        own[:, cols] = value + tok[:, cols].astype(F32)

    multiply(3, store_own)
    for p in range(PIECES):
        for way in range(2):
            near_copy(p, way, 0).wait_recv()
            near_copy(p, way, 1).wait_recv()
        part = pl.ds(p * size, size)
        total = from_left[part, :].astype(F32) + from_right[part, :].astype(F32)
        section[part, :] = (own[part, :] + total).astype(BF16)
        go(remote(section.at[part], out.at[part], x, p, {"pipe": ahead}))
    for p in range(PIECES):
        part = pl.ds(p * size, size)
        remote(section.at[part], out.at[part], x, p, {"pipe": ahead}).wait_recv()
    for copy in started:
        copy.wait_send()


def output(att, own_rows, w_out, n_pipe, n_t):
    rows, width = own_rows.shape
    vmem = pl.BlockSpec(memory_space=pltpu.VMEM)
    anywhere = pl.BlockSpec(memory_space=pl.ANY)
    whole = (rows, width)
    return pl.pallas_call(
        functools.partial(output_kernel, n_pipe, n_t),
        out_shape=jax.ShapeDtypeStruct(whole, BF16),
        in_specs=[vmem, vmem, anywhere],
        out_specs=anywhere,
        scratch_shapes=[
            pltpu.VMEM((n_t, w_out.shape[0], width), BF16),
            pltpu.VMEM(whole, BF16),
            pltpu.VMEM(whole, BF16),
            pltpu.VMEM(whole, F32),
            pltpu.VMEM(whole, F32),
            pltpu.VMEM(whole, F32),
            pltpu.VMEM((2,) + whole, BF16),
            pltpu.VMEM(whole, BF16),
            pltpu.VMEM(whole, BF16),
            pltpu.VMEM(whole, BF16),
            pltpu.SemaphoreType.DMA((n_t,)),
            pltpu.SemaphoreType.DMA((6 * PIECES,)),
            pltpu.SemaphoreType.DMA((6 * PIECES,)),
            pltpu.SemaphoreType.DMA((PIECES,)),
            pltpu.SemaphoreType.DMA((PIECES,)),
        ],
        compiler_params=pltpu.CompilerParams(
            collective_id=1, has_side_effects=True, vmem_limit_bytes=40 * 1024 * 1024
        ),
        name="output",
    )(att, own_rows, w_out)


def on_device(
    tokens, norm_gain, w_query, key_value_weight, w_out, cache_kv,
    cache_lengths, row_lengths, block_owner,
):
    n_pipe, n_dp, n_t = (lax.axis_size(a) for a in ("pipe", "dp", "tensor"))
    own_rows = tokens[0]
    span = cache_kv.shape[1]
    cache = cache_kv.reshape(span, cache_kv.shape[3])
    q, kv_full, cache_full = project(
        own_rows, norm_gain, w_query[0], key_value_weight[0], cache, n_dp, n_t
    )
    kv_width = kv_full.shape[2]
    att, held = attend(
        cache_lengths, row_lengths, block_owner.reshape(-1), q,
        cache_full.reshape(-1, kv_width), kv_full.reshape(-1, kv_width),
    )
    handed = output(att, own_rows, w_out[0], n_pipe, n_t)
    return handed[None], held


def solution(mesh):
    placed = (
        P("pipe", "dp", "tensor"),
        P("pipe", None),
        P("pipe", None, "tensor"),
        P("pipe", None, "tensor"),
        P("pipe", "tensor", None),
        P("pipe", "dp", "tensor", None),
        P("pipe", None),
        P("pipe", None),
        P("pipe", None, None),
    )
    return jax.shard_map(
        on_device,
        mesh=mesh,
        in_specs=placed,
        out_specs=(P("pipe", "dp", "tensor"), P("pipe", "dp")),
        check_vma=False,
    )
```

time: 989 us -> 123 us (0.12)
  the two profiles are of different devices: /device:TPU:8 before, /device:TPU:16 now
where the time goes in v1:
time: 123 us
  Pallas kernels  116 us (94%)
  local copies, waits for them, and re-layouts  5.82 us (5%)
    pallas_call x1, Pallas kernels, output(): pl.pallas_call(functools.partial(output_kernel, n_pipe, n_t), out_shape=j...  55.1 us
    pallas_call x1, Pallas kernels, project(): pl.pallas_call(functools.partial(project_kernel, n_dp, n_t), out_shape=(j...  38.7 us
    pallas_call x1, Pallas kernels, attend(): pl.pallas_call(functools.partial(attend_kernel, cache_len.shape[1]), out_...  22.4 us
    unnamed x23, local copies, waits for them, and re-layouts  5.82 us

profile of v1, /device:TPU:16, one launch (start us, length us, event | category | flops | bytes accessed | tf_op | source)
XLA Modules:
  0.0 122.9 jit_solution(2892828053869084409)
XLA Ops:
  0.6 0.0 slice-start
  0.6 0.0 copy-start
  0.7 1.2 copy-done
  1.9 0.0 copy-start.2
  1.9 1.9 %copy-done.2 = bf16[1,5120,256]{2,1,0:T(8,128)(2,1)S(1)} copy-done((bf16[1,5120,256]{2,1,0:T(8,128)(2,1)S(1)}, bf16[1,5120,256]{2,1,0:T(8,128)(2,1)}, u32[]{:S(2)}) %copy-start.2) | copy-done | bytes 2621464
  3.8 0.0 copy-start.3
  3.8 1.0 copy-done.3
  4.9 0.0 copy-start.4
  4.9 0.7 copy-done.4
  5.6 0.0 copy-start.5
  5.6 0.0 copy-start.6
  5.6 0.0 copy-start.7
  5.6 0.0 slice-start.1
  5.6 0.0 slice-start.2
  5.6 0.0 copy-start.1
  5.6 38.7 %project.1 = (bf16[2,8,128,128]{3,2,1,0:T(8,128)(2,1)S(1)}, bf16[8,256,256]{2,1,0:T(8,128)(2,1)S(1)}, bf16[8,1024,256]{2,1,0:T(8,128)(2,1)S(1)}) custom-call(bf16[256,1280]{1,0:T(8,128)(2,1)S(1)} %bitcast.13, bf16[1,5120]{1,0:T(2,128)(2,1)S(1)} %copy-done.4, bf16[5120,1024]{1,0:T(8,128)(2,1)} %bitcast.20, bf16[5120,256]{1,0:T(8,128)(2,1)S(1)} %bitcast.16, ...), custom_call_target="tpu_custom_call" | custom-call | tf_op jit(solution)/shard_map/project/pallas_call | solution.py:200
  44.4 0.0 copy-done.5
  44.4 0.0 copy-done.6
  44.4 0.0 copy-done.7
  44.4 22.4 %attend.1 = (bf16[256,1024]{1,0:T(8,128)(2,1)S(1)}, f32[1,1]{1,0:T(1,128)}) custom-call(s32[1,4]{1,0:T(1,128)S(1)} %copy-done.5, s32[1,4]{1,0:T(1,128)S(1)} %copy-done.6, s32[16]{0:T(128)S(1)} %bitcast.19, bf16[2,8,128,128]{3,2,1,0:T(8,128)(2,1)S(1)} %get-tuple-element.7.q, bf16[8192,256]{1,0:T(8,128)(2,1)S(1)} %bitcast.12, bf16[2048,256]{1,0:T(8,128)(2,1)S(1)} %bitcast.17), custom_call_target="tpu_custom_call" | custom-call | tf_op jit(solution)/shard_map/attend/pallas_call | solution.py:353
  66.8 0.0 slice-done
  66.9 0.0 slice-done.1
  66.9 0.0 slice-done.2
  66.9 0.0 copy-done.1
  66.9 55.1 %output.1 = bf16[256,1280]{1,0:T(8,128)(2,1)S(1)} custom-call(bf16[256,1024]{1,0:T(8,128)(2,1)S(1)} %get-tuple-element.10.att, bf16[256,1280]{1,0:T(8,128)(2,1)S(1)} %bitcast.14, bf16[1024,5120]{1,0:T(8,128)(2,1)S(1)} %bitcast.11), custom_call_target="tpu_custom_call" | custom-call | tf_op jit(solution)/shard_map/output/pallas_call | solution.py:483
  122.0 0.8 copy.12
  (1 shorter events, 0.0 us)
Async XLA Ops:
  0.6 66.2 %slice-start = ((s8[10485760]{0:T(1024)(128)(4,1)}), s8[4194304]{0:T(1024)(128)(4,1)S(1)}, s32[]{:S(2)}) async-start(s8[10485760]{0:T(1024)(128)(4,1)} %bitcast.9), calls=%async_computation | async-start | bytes 8388608
  0.6 1.2 %copy-start = (bf16[1,256,1280]{2,1,0:T(8,128)(2,1)S(1)}, bf16[1,256,1280]{2,1,0:T(8,128)(2,1)}, u32[]{:S(2)}) copy-start(bf16[1,256,1280]{2,1,0:T(8,128)(2,1)} %param.9) | copy-start | bytes 1966084
  1.9 1.9 %copy-start.2 = (bf16[1,5120,256]{2,1,0:T(8,128)(2,1)S(1)}, bf16[1,5120,256]{2,1,0:T(8,128)(2,1)}, u32[]{:S(2)}) copy-start(bf16[1,5120,256]{2,1,0:T(8,128)(2,1)} %param.12) | copy-start | bytes 7864324
  3.8 1.0 copy-start.3
  4.9 0.7 copy-start.4
  5.6 38.8 %copy-start.5 = (s32[1,4]{1,0:T(1,128)S(1)}, s32[1,4]{1,0:T(1,128)}, u32[]{:S(2)}) copy-start(s32[1,4]{1,0:T(1,128)} %cache_len.1) | copy-start | bytes 52
  5.6 38.8 %copy-start.6 = (s32[1,4]{1,0:T(1,128)S(1)}, s32[1,4]{1,0:T(1,128)}, u32[]{:S(2)}) copy-start(s32[1,4]{1,0:T(1,128)} %row_len.1) | copy-start | bytes 52
  5.6 38.8 %copy-start.7 = (s32[1,16,1]{1,2,0:T(1,128)S(1)}, s32[1,16,1]{1,2,0:T(1,128)}, u32[]{:S(2)}) copy-start(s32[1,16,1]{1,2,0:T(1,128)} %param.17) | copy-start | bytes 196
  5.6 61.3 %slice-start.1 = ((s8[10485760]{0:T(1024)(128)(4,1)}), s8[4194304]{0:T(1024)(128)(4,1)S(1)}, s32[]{:S(2)}) async-start(s8[10485760]{0:T(1024)(128)(4,1)} %bitcast.9), calls=%async_computation.1 | async-start | bytes 8388608
  5.6 61.3 %slice-start.2 = ((s8[10485760]{0:T(1024)(128)(4,1)}), s8[2097152]{0:T(1024)(128)(4,1)S(1)}, s32[]{:S(2)}) async-start(s8[10485760]{0:T(1024)(128)(4,1)} %bitcast.9), calls=%async_computation.2 | async-start | bytes 4194304
  5.6 61.3 %copy-start.1 = (bf16[1,256,1280]{2,1,0:T(8,128)(2,1)S(1)}, bf16[1,256,1280]{2,1,0:T(8,128)(2,1)}, u32[]{:S(2)}) copy-start(bf16[1,256,1280]{2,1,0:T(8,128)(2,1)} %param.9) | copy-start | bytes 1966084

commit v2 on v1

v2 whole, which is shorter than its diff:
```python
import functools

import jax
import jax.numpy as jnp
from jax import lax
from jax.experimental import pallas as pl
from jax.experimental.pallas import tpu as pltpu
from jax.sharding import PartitionSpec as P

HEAD = 128
BLOCK = 128
EPS = 1e-06
NEG = -1e30
LOG2E = 1.4426950408889634
MESH = pl.DeviceIdType.MESH
F32 = jnp.float32
BF16 = jnp.bfloat16


def remote(src, dst, sems, index, target):
    return pltpu.make_async_remote_copy(
        src_ref=src,
        dst_ref=dst,
        send_sem=sems[0].at[index],
        recv_sem=sems[1].at[index],
        device_id=target,
        device_id_type=MESH,
    )


def project_kernel(
    n_dp, n_t, tok, gain_hbm, wq_hbm, wkv_hbm, cache, q_out, hist,
    xs, gain, wq, wkv, normed, kv_own, w_sem, loc_sem,
    z_send, z_recv, y_send, y_recv, k_send, k_recv,
):
    rank = lax.axis_index("dp")
    t = lax.axis_index("tensor")
    right, left = lax.rem(t + 1, n_t), lax.rem(t + n_t - 1, n_t)
    over = lax.rem(t + 2, n_t)
    up, down = lax.rem(rank + 2, n_dp), lax.rem(rank + n_dp - 2, n_dp)
    across = lax.rem(rank + 4, n_dp)
    twin = rank + 1 - 2 * lax.rem(rank, 2)
    z, y, k = (z_send, z_recv), (y_send, y_recv), (k_send, k_recv)
    half = BLOCK // 2
    span = cache.shape[0]
    mid = span // 2
    fresh = span * n_dp

    def cached_at(slot, lower, upper):
        return hist.at[pl.ds(pl.multiple_of(slot * span + lower, mid), upper - lower)]

    def fresh_at(slot, lower, upper):
        place = fresh + slot * kv_own.shape[0] + lower
        return hist.at[pl.ds(pl.multiple_of(place, BLOCK), upper - lower)]

    w_copies = [
        pltpu.make_async_copy(wq_hbm, wq, w_sem.at[0]),
        pltpu.make_async_copy(wkv_hbm, wkv, w_sem.at[1]),
        pltpu.make_async_copy(gain_hbm, gain, w_sem.at[2]),
    ]

    barrier = pltpu.get_barrier_semaphore()
    for other in (left, right):
        pl.semaphore_signal(barrier, inc=1, device_id={"tensor": other}, device_id_type=MESH)
    for step in range(1, n_dp):
        other = lax.rem(rank + step, n_dp)
        pl.semaphore_signal(barrier, inc=1, device_id={"dp": other}, device_id_type=MESH)
    pl.semaphore_wait(barrier, 2 + n_dp - 1)

    def rows(block, lower, upper):
        return pl.ds(block * BLOCK + lower, upper - lower)

    def z_own(block, way, target):
        part = rows(block, 0, BLOCK)
        return remote(tok.at[part], xs.at[t, part], z, block * 4 + way, {"tensor": target})

    def z_own_in(block, way, source):
        part = xs.at[source, rows(block, 0, BLOCK)]
        return remote(part, part, z, block * 4 + way, {"tensor": source})

    def z_far(block, way, slot, target):
        low = 0 if way == 0 else half
        part = xs.at[slot, rows(block, low, low + half)]
        return remote(part, part, z, block * 4 + 2 + way, {"tensor": target})

    started = []

    def go(copy):
        copy.start()
        started.append(copy)

    go(z_own(0, 0, right))
    go(z_own(0, 1, left))
    go(remote(cache, cached_at(rank, 0, span), y, 0, {"dp": up}))
    go(remote(cache, cached_at(rank, 0, span), y, 1, {"dp": down}))
    go(remote(cache, cached_at(rank, 0, span), y, 4, {"dp": twin}))
    own_cache = pltpu.make_async_copy(cache, cached_at(rank, 0, span), loc_sem.at[0])
    own_cache.start()
    for copy in w_copies:
        copy.start()
    own_tok = pltpu.make_async_copy(tok, xs.at[t], loc_sem.at[2])
    own_tok.start()

    def y_in(index, slot, lower, upper):
        part = cached_at(slot, lower, upper)
        return remote(part, part, y, index, {"dp": twin})

    def y_out(index, slot, lower, upper, target):
        part = cached_at(slot, lower, upper)
        go(remote(part, part, y, index, {"dp": target}))

    def forward_z(block):
        z_own_in(block, 0, left).wait_recv()
        go(z_far(block, 0, left, right))
        z_own_in(block, 1, right).wait_recv()
        go(z_far(block, 1, right, left))

    def far_z(block):
        z_far(block, 0, over, right).wait_recv()
        z_far(block, 1, over, left).wait_recv()

    def compute(block):
        def norm_rows(step, carry):
            low = pl.multiple_of(block * BLOCK + step * 16, 16)
            low_here = pl.multiple_of(step * 16, 16)
            parts = [xs[i, pl.ds(low, 16), :].astype(F32) for i in range(n_t)]
            total = jnp.sum(parts[0] * parts[0], axis=1, keepdims=True)
            for part in parts[1:]:
                total += jnp.sum(part * part, axis=1, keepdims=True)
            width = parts[0].shape[1]
            factor = lax.rsqrt(total / (width * n_t) + EPS)
            for i, part in enumerate(parts):
                cols = pl.ds(i * width, width)
                scaled = part * factor * gain[:, cols].astype(F32)
                normed[pl.ds(low_here, 16), cols] = scaled.astype(BF16)
            return carry

        if block == 0:
            w_copies[2].wait()
        lax.fori_loop(0, BLOCK // 16, norm_rows, 0)

        if block == 0:
            w_copies[1].wait()
        made = jnp.dot(normed[...], wkv[...], preferred_element_type=F32)
        kv_own[pl.ds(block * BLOCK, BLOCK), :] = made.astype(BF16)
        part = pl.ds(block * BLOCK, BLOCK)
        for step in range(1, n_dp):
            other = lax.rem(rank + step, n_dp)
            index = block * (n_dp - 1) + step - 1
            here = fresh_at(rank, block * BLOCK, block * BLOCK + BLOCK)
            go(remote(kv_own.at[part], here, k, index, {"dp": other}))
        if block == 0:
            w_copies[0].wait()

        def query_tile(n, carry):
            cols = pl.ds(pl.multiple_of(n * 256, 256), 256)
            tile = jnp.dot(normed[...], wq[:, cols], preferred_element_type=F32).astype(BF16)
            q_out[block, 2 * n] = tile[:, :HEAD]
            q_out[block, 2 * n + 1] = tile[:, HEAD:]
            return carry

        lax.fori_loop(0, wq.shape[1] // 256, query_tile, 0)

    forward_z(0)
    own_tok.wait()
    go(z_own(1, 0, right))
    go(z_own(1, 1, left))
    far_z(0)
    y_in(0, down, 0, span).wait_recv()
    y_out(2, down, 0, mid, up)
    y_out(5, down, 0, span, twin)
    y_in(1, up, 0, span).wait_recv()
    y_out(3, up, mid, span, down)
    y_out(6, up, 0, span, twin)
    compute(0)
    forward_z(1)
    y_in(2, across, 0, mid).wait_recv()
    y_out(7, across, 0, mid, twin)
    y_in(3, across, mid, span).wait_recv()
    y_out(8, across, mid, span, twin)
    far_z(1)
    compute(1)

    own_kv = pltpu.make_async_copy(kv_own, fresh_at(rank, 0, kv_own.shape[0]), loc_sem.at[1])
    own_kv.start()
    twin_of = lambda r: r + 1 - 2 * lax.rem(r, 2)
    y_in(4, twin, 0, span).wait_recv()
    y_in(5, twin_of(down), 0, span).wait_recv()
    y_in(6, twin_of(up), 0, span).wait_recv()
    y_in(7, twin_of(across), 0, mid).wait_recv()
    y_in(8, twin_of(across), mid, span).wait_recv()
    for block in range(2):
        for step in range(1, n_dp):
            source = lax.rem(rank + n_dp - step, n_dp)
            index = block * (n_dp - 1) + step - 1
            here = fresh_at(source, block * BLOCK, block * BLOCK + BLOCK)
            remote(here, here, k, index, {"dp": source}).wait_recv()
    own_cache.wait()
    own_kv.wait()
    for copy in started:
        copy.wait_send()


def project(own_rows, gain, w_query, w_kv, cache, n_dp, n_t):
    rows, width = own_rows.shape
    blocks = rows // BLOCK
    full, heads_width = w_query.shape
    kv_width = w_kv.shape[1]
    heads = heads_width // HEAD
    span = cache.shape[0]
    vmem = pl.BlockSpec(memory_space=pltpu.VMEM)
    hbm = pl.BlockSpec(memory_space=pltpu.HBM)
    return pl.pallas_call(
        functools.partial(project_kernel, n_dp, n_t),
        out_shape=(
            jax.ShapeDtypeStruct((blocks, heads, BLOCK, HEAD), BF16),
            jax.ShapeDtypeStruct((n_dp * (span + rows), kv_width), BF16),
        ),
        in_specs=[hbm] * 5,
        out_specs=(vmem, pl.BlockSpec(memory_space=pltpu.VMEM)),
        scratch_shapes=[
            pltpu.VMEM((n_t, rows, width), BF16),
            pltpu.VMEM(gain.shape, BF16),
            pltpu.VMEM((full, heads_width), BF16),
            pltpu.VMEM((full, kv_width), BF16),
            pltpu.VMEM((BLOCK, full), BF16),
            pltpu.VMEM((rows, kv_width), BF16),
            pltpu.SemaphoreType.DMA((3,)),
            pltpu.SemaphoreType.DMA((3,)),
            pltpu.SemaphoreType.DMA((8,)),
            pltpu.SemaphoreType.DMA((8,)),
            pltpu.SemaphoreType.DMA((9,)),
            pltpu.SemaphoreType.DMA((9,)),
            pltpu.SemaphoreType.DMA((2 * (n_dp - 1),)),
            pltpu.SemaphoreType.DMA((2 * (n_dp - 1),)),
        ],
        compiler_params=pltpu.CompilerParams(
            collective_id=0, has_side_effects=True, vmem_limit_bytes=40 * 1024 * 1024
        ),
        name="project",
    )(*(pltpu.with_memory_space_constraint(a, pltpu.HBM) for a in (own_rows, gain, w_query, w_kv, cache)))


class Layout:
    def __init__(self, cache_len, row_len, n_docs):
        self.n = n_docs
        self.c_len = [cache_len[0, d] for d in range(n_docs)]
        self.r_len = [row_len[0, d] for d in range(n_docs)]
        self.r_start, self.r_end = [], []
        total = jnp.int32(0)
        for length in self.r_len:
            self.r_start.append(total)
            total = total + length
            self.r_end.append(total)

    def _sum(self, tests, values):
        total = jnp.where(tests[0], values[0], 0)
        for test, value in zip(tests[1:], values[1:]):
            total = total + jnp.where(test, value, 0)
        return total

    def ranges(self, first, last):
        past = [end <= first for end in self.r_end]
        begun = [start <= last for start in self.r_start]
        return self._sum(past, self.c_len), self._sum(begun, self.c_len), self._sum(past, self.r_len)


def lane_rows(first):
    return first + lax.broadcasted_iota(jnp.int32, (1, BLOCK), 1)


def align_down(value):
    return value // 16 * 16


def reset_state(m_s, l_s, acc_s):
    m_s[...] = jnp.full(m_s.shape, NEG, F32)
    l_s[...] = jnp.zeros(l_s.shape, F32)
    acc_s[...] = jnp.zeros(acc_s.shape, F32)


def attend_chunk(hist, start, size, low, high, queries, m_s, l_s, acc_s):
    scale = HEAD ** (-0.5) * LOG2E
    place0 = jnp.minimum(start, hist.shape[0] - size)
    at = pl.ds(pl.multiple_of(place0, 16), size)
    keys = hist[at, :HEAD]
    values_t = hist[at, HEAD:].T
    place = place0 + lax.broadcasted_iota(jnp.int32, (size, BLOCK), 0)
    bias = jnp.where((place >= jnp.maximum(low, start)) & (place < high), 0.0, 2 * NEG)
    bias = jnp.concatenate([bias, bias], axis=1)
    heads = len(queries)
    scores = []
    for h in range(0, heads, 2):
        pair = jnp.concatenate([queries[h], queries[h + 1]], axis=0)
        scores.append(
            lax.dot_general(keys, pair, (((1,), (1,)), ((), ())), preferred_element_type=F32)
        )
    weighted = []
    for i, score in enumerate(scores):
        cols = pl.ds(i * 2 * BLOCK, 2 * BLOCK)
        score = score + bias
        prior = m_s[:, cols]
        newest = jnp.maximum(prior, jnp.max(score, axis=0, keepdims=True))
        weights = jnp.exp2((score - newest) * scale)
        rescale = jnp.exp2((prior - newest) * scale)
        m_s[:, cols] = newest
        l_s[:, cols] = l_s[:, cols] * rescale + jnp.sum(weights, axis=0, keepdims=True)
        weighted.append((weights.astype(BF16), rescale))
    for i, (weights, rescale) in enumerate(weighted):
        cols = pl.ds(i * 2 * BLOCK, 2 * BLOCK)
        product = jnp.dot(values_t, weights, preferred_element_type=F32)
        acc_s[:, cols] = acc_s[:, cols] * rescale + product


def finish_block(heads, m_s, l_s, acc_s, store):
    for h in range(heads):
        cols = pl.ds(h * BLOCK, BLOCK)
        store(cols, (acc_s[:, cols] / l_s[:, cols]).T.astype(BF16))


CHUNK = 1024


def attend_kernel(
    n_docs, cached, cache_len, row_len, owner, q, hist, out, held, m_s, l_s, acc_s
):
    rank = lax.axis_index("dp")
    blocks, heads = q.shape[:2]
    layout = Layout(cache_len, row_len, n_docs)

    def one_block(block, carry):
        first = (rank * blocks + block) * BLOCK
        c_low, c_high, r_low = layout.ranges(first, first + BLOCK - 1)
        row = lane_rows(first)
        row_c_low, row_c_high, row_r_low = layout.ranges(row, row)
        reset_state(m_s, l_s, acc_s)
        queries = [q[block, h] for h in range(heads)]

        def one_range(part, carry):
            new = part == 1
            low = jnp.where(new, cached + r_low, c_low)
            high = jnp.where(new, cached + first + BLOCK, c_high)
            lane_low = jnp.where(new, cached + row_r_low, row_c_low)
            lane_high = jnp.where(new, cached + row + 1, row_c_high)
            begin = align_down(low)
            total = high - begin
            whole = total // CHUNK
            rest = total - whole * CHUNK

            def one(k, carry):
                attend_chunk(
                    hist, begin + k * CHUNK, CHUNK, lane_low, lane_high, queries, m_s, l_s, acc_s
                )
                return carry

            lax.fori_loop(0, whole + (rest > CHUNK // 2).astype(jnp.int32), one, 0)

            @pl.when((rest > 0) & (rest <= CHUNK // 2))
            def _():
                attend_chunk(
                    hist, begin + whole * CHUNK, CHUNK // 2, lane_low, lane_high, queries,
                    m_s, l_s, acc_s,
                )

            return carry

        lax.fori_loop(0, 2, one_range, 0)

        def store(cols, value):
            out[pl.ds(pl.multiple_of(block * BLOCK, BLOCK), BLOCK), cols] = value

        finish_block(heads, m_s, l_s, acc_s, store)
        return carry

    lax.fori_loop(0, blocks, one_block, 0)

    def load_of(b, total):
        low = b * BLOCK
        work = low * BLOCK + (BLOCK * (BLOCK - 1)) // 2
        for d in range(n_docs):
            inside = jnp.minimum(layout.r_end[d], low + BLOCK) - jnp.maximum(layout.r_start[d], low)
            gain = layout.c_len[d] - layout.r_start[d] + 1
            work = work + jnp.maximum(inside, 0) * gain
        return total + jnp.where(owner[b] == rank, work, 0)

    total = lax.fori_loop(0, owner.shape[0], load_of, jnp.int32(0))
    held[0, 0] = total.astype(F32) * (1.0 / (BLOCK * (hist.shape[0] // 2)))


def attend(cache_len, row_len, owner, q, hist, cached):
    blocks, heads = q.shape[:2]
    vmem = pl.BlockSpec(memory_space=pltpu.VMEM)
    smem = pl.BlockSpec(memory_space=pltpu.SMEM)
    return pl.pallas_call(
        functools.partial(attend_kernel, cache_len.shape[1], cached),
        out_shape=(
            jax.ShapeDtypeStruct((blocks * BLOCK, heads * HEAD), BF16),
            jax.ShapeDtypeStruct((1, 1), F32),
        ),
        in_specs=[smem, smem, smem, vmem, vmem],
        out_specs=(vmem, smem),
        scratch_shapes=[
            pltpu.VMEM((1, heads * BLOCK), F32),
            pltpu.VMEM((1, heads * BLOCK), F32),
            pltpu.VMEM((HEAD, heads * BLOCK), F32),
        ],
        compiler_params=pltpu.CompilerParams(vmem_limit_bytes=40 * 1024 * 1024),
        name="attend",
    )(cache_len, row_len, owner, q, hist)


PIECES = 4


def output_kernel(
    n_pipe, n_t, att, tok, wo, out,
    far, far_in, to_right, to_left, own, sent, from_left, from_right, section,
    z_send, z_recv, x_send, x_recv,
):
    s = lax.axis_index("pipe")
    t = lax.axis_index("tensor")
    right, left = lax.rem(t + 1, n_t), lax.rem(t + n_t - 1, n_t)
    over = lax.rem(t + 2, n_t)
    ahead, behind = lax.rem(s + 1, n_pipe), lax.rem(s + n_pipe - 1, n_pipe)
    z, x = (z_send, z_recv), (x_send, x_recv)
    width = tok.shape[1]
    size = tok.shape[0] // PIECES
    half = size // 2
    barrier = pltpu.get_barrier_semaphore()
    for other in (left, right):
        pl.semaphore_signal(barrier, inc=1, device_id={"tensor": other}, device_id_type=MESH)
    for other in (ahead, behind):
        pl.semaphore_signal(barrier, inc=1, device_id={"pipe": other}, device_id_type=MESH)
    pl.semaphore_wait(barrier, 4)

    def multiply(target, store):
        def tile(n, carry):
            cols = pl.ds(pl.multiple_of(n * 256, 256), 256)
            out_cols = pl.ds(pl.multiple_of(target * width + n * 256, 256), 256)
            store(cols, jnp.dot(att[...], wo[:, out_cols], preferred_element_type=F32))
            return carry

        lax.fori_loop(0, width // 256, tile, 0)

    started = []

    def go(copy):
        copy.start()
        started.append(copy)

    def span(p, way):
        return pl.ds(p * size + way * half, half)

    def far_copy(p, way):
        target = right if way == 0 else left
        return remote(far.at[span(p, way)], far_in.at[span(p, way)], z, p * 6 + way, {"tensor": target})

    def near_copy(p, way, kind):
        part = span(p, way if kind == 1 else 1 - way)
        target, box = (right, from_left) if way == 0 else (left, from_right)
        return remote(sent.at[way, part], box.at[part], z, p * 6 + 2 + 2 * kind + way, {"tensor": target})

    def store_far(cols, value):
        far[:, cols] = value.astype(BF16)

    multiply(over, store_far)
    for p in range(PIECES):
        for way in range(2):
            go(far_copy(p, way))

    def store_right(cols, value):
        to_right[:, cols] = value

    def store_left(cols, value):
        to_left[:, cols] = value

    multiply(right, store_right)
    multiply(left, store_left)
    held = (to_right, to_left)
    for p in range(PIECES):
        for way in range(2):
            part = span(p, 1 - way)
            sent[way, part, :] = held[way][part, :].astype(BF16)
            go(near_copy(p, way, 0))
        for way in range(2):
            part = span(p, way)
            far_copy(p, way).wait_recv()
            sent[way, part, :] = (held[way][part, :] + far_in[part, :].astype(F32)).astype(BF16)
            go(near_copy(p, way, 1))

    def store_own(cols, value):
        own[:, cols] = value + tok[:, cols].astype(F32)

    multiply(t, store_own)
    for p in range(PIECES):
        for way in range(2):
            near_copy(p, way, 0).wait_recv()
            near_copy(p, way, 1).wait_recv()
        part = pl.ds(p * size, size)
        total = from_left[part, :].astype(F32) + from_right[part, :].astype(F32)
        section[part, :] = (own[part, :] + total).astype(BF16)
        go(remote(section.at[part], out.at[part], x, p, {"pipe": ahead}))
    for p in range(PIECES):
        part = pl.ds(p * size, size)
        remote(section.at[part], out.at[part], x, p, {"pipe": ahead}).wait_recv()
    for copy in started:
        copy.wait_send()


def output(att, own_rows, w_out, n_pipe, n_t):
    rows, width = own_rows.shape
    vmem = pl.BlockSpec(memory_space=pltpu.VMEM)
    anywhere = pl.BlockSpec(memory_space=pl.ANY)
    whole = (rows, width)
    return pl.pallas_call(
        functools.partial(output_kernel, n_pipe, n_t),
        out_shape=jax.ShapeDtypeStruct(whole, BF16),
        in_specs=[vmem, vmem, vmem],
        out_specs=anywhere,
        scratch_shapes=[
            pltpu.VMEM(whole, BF16),
            pltpu.VMEM(whole, BF16),
            pltpu.VMEM(whole, F32),
            pltpu.VMEM(whole, F32),
            pltpu.VMEM(whole, F32),
            pltpu.VMEM((2,) + whole, BF16),
            pltpu.VMEM(whole, BF16),
            pltpu.VMEM(whole, BF16),
            pltpu.VMEM(whole, BF16),
            pltpu.SemaphoreType.DMA((6 * PIECES,)),
            pltpu.SemaphoreType.DMA((6 * PIECES,)),
            pltpu.SemaphoreType.DMA((PIECES,)),
            pltpu.SemaphoreType.DMA((PIECES,)),
        ],
        compiler_params=pltpu.CompilerParams(
            collective_id=1, has_side_effects=True, vmem_limit_bytes=40 * 1024 * 1024
        ),
        name="output",
    )(att, own_rows, w_out)


def on_device(
    tokens, norm_gain, w_query, key_value_weight, w_out, cache_kv,
    cache_lengths, row_lengths, block_owner,
):
    n_pipe, n_dp, n_t = (lax.axis_size(a) for a in ("pipe", "dp", "tensor"))
    own_rows = tokens[0]
    span = cache_kv.shape[1]
    cache = cache_kv.reshape(span, cache_kv.shape[3])
    q, hist = project(
        own_rows, norm_gain, w_query[0], key_value_weight[0], cache, n_dp, n_t
    )
    att, held = attend(
        cache_lengths, row_lengths, block_owner.reshape(-1), q, hist, span * n_dp
    )
    handed = output(att, own_rows, w_out[0], n_pipe, n_t)
    return handed[None], held


def solution(mesh):
    placed = (
        P("pipe", "dp", "tensor"),
        P("pipe", None),
        P("pipe", None, "tensor"),
        P("pipe", None, "tensor"),
        P("pipe", "tensor", None),
        P("pipe", "dp", "tensor", None),
        P("pipe", None),
        P("pipe", None),
        P("pipe", None, None),
    )
    return jax.shard_map(
        on_device,
        mesh=mesh,
        in_specs=placed,
        out_specs=(P("pipe", "dp", "tensor"), P("pipe", "dp")),
        check_vma=False,
    )
```

time: 123 us -> 95 us (0.77)
  the two profiles are of different devices: /device:TPU:16 before, /device:TPU:8 now
where the time goes in v2:
time: 95 us; the launch traced here: 94.7 us
  Pallas kernels  93 us (98%)
    pallas_call x1, Pallas kernels, project(): pl.pallas_call(functools.partial(project_kernel, n_dp, n_t), out_shape=(j...  37.9 us
    pallas_call x1, Pallas kernels, output(): pl.pallas_call(functools.partial(output_kernel, n_pipe, n_t), out_shape=j...  34.3 us
    pallas_call x1, Pallas kernels, attend(): pl.pallas_call(functools.partial(attend_kernel, cache_len.shape[1], cache...  20.8 us

profile of v2, /device:TPU:8, one launch (start us, length us, event | category | flops | bytes accessed | tf_op | source)
XLA Modules:
  0.0 94.7 jit_solution(4101725424690059377)
XLA Ops:
  0.6 0.0 copy-start.3
  0.6 0.0 copy-start.2
  0.7 0.0 copy-start.1
  0.7 0.0 slice-start
  0.7 0.0 copy-start
  0.7 0.0 slice-start.1
  0.7 0.0 slice-start.2
  0.7 37.9 %project.1 = (bf16[2,8,128,128]{3,2,1,0:T(8,128)(2,1)S(1)}, bf16[10240,256]{1,0:T(8,128)(2,1)S(1)}) custom-call(bf16[256,1280]{1,0:T(8,128)(2,1)} %bitcast.10, bf16[1,5120]{1,0:T(2,128)(2,1)} %gain_hbm.1, bf16[5120,1024]{1,0:T(8,128)(2,1)} %bitcast.14, bf16[5120,256]{1,0:T(8,128)(2,1)} %bitcast.15, bf16[1024,256]{1,0:T(8,128)(2,1)} %bitcast.16), custom_call_target="tpu_custom_call" | custom-call | tf_op jit(solution)/shard_map/project/pallas_call | solution.py:213
  38.7 0.0 copy-done.3
  38.7 0.0 copy-done.2
  38.7 0.0 copy-done.1
  38.7 20.8 %attend.1 = (bf16[256,1024]{1,0:T(8,128)(2,1)S(1)}, f32[1,1]{1,0:T(1,128)}) custom-call(s32[1,4]{1,0:T(1,128)S(1)} %copy-done.1, s32[1,4]{1,0:T(1,128)S(1)} %copy-done.2, s32[16]{0:T(128)S(1)} %bitcast.13, bf16[2,8,128,128]{3,2,1,0:T(8,128)(2,1)S(1)} %get-tuple-element.6.q, bf16[10240,256]{1,0:T(8,128)(2,1)S(1)} %get-tuple-element.7.hist), custom_call_target="tpu_custom_call" | custom-call | tf_op jit(solution)/shard_map/attend/pallas_call | solution.py:394
  59.5 0.0 slice-done
  59.5 0.0 copy-done
  59.5 0.0 slice-done.1
  59.5 0.0 slice-done.2
  59.5 34.3 %output.1 = bf16[256,1280]{1,0:T(8,128)(2,1)S(1)} custom-call(bf16[256,1024]{1,0:T(8,128)(2,1)S(1)} %get-tuple-element.8.att, bf16[256,1280]{1,0:T(8,128)(2,1)S(1)} %bitcast.11, bf16[1024,5120]{1,0:T(8,128)(2,1)S(1)} %bitcast.9), custom_call_target="tpu_custom_call" | custom-call | tf_op jit(solution)/shard_map/output/pallas_call | solution.py:515
  93.8 0.8 copy.12
  (1 shorter events, 0.0 us)
Async XLA Ops:
  0.6 38.0 %copy-start.3 = (s32[1,16,1]{1,2,0:T(1,128)S(1)}, s32[1,16,1]{1,2,0:T(1,128)}, u32[]{:S(2)}) copy-start(s32[1,16,1]{1,2,0:T(1,128)} %param.17) | copy-start | bytes 196
  0.6 38.0 %copy-start.2 = (s32[1,4]{1,0:T(1,128)S(1)}, s32[1,4]{1,0:T(1,128)}, u32[]{:S(2)}) copy-start(s32[1,4]{1,0:T(1,128)} %row_len.1) | copy-start | bytes 52
  0.7 38.0 %copy-start.1 = (s32[1,4]{1,0:T(1,128)S(1)}, s32[1,4]{1,0:T(1,128)}, u32[]{:S(2)}) copy-start(s32[1,4]{1,0:T(1,128)} %cache_len.1) | copy-start | bytes 52
  0.7 58.8 %slice-start = ((s8[10485760]{0:T(1024)(128)(4,1)}), s8[4194304]{0:T(1024)(128)(4,1)S(1)}, s32[]{:S(2)}) async-start(s8[10485760]{0:T(1024)(128)(4,1)} %bitcast.7), calls=%async_computation | async-start | bytes 8388608
  0.7 58.8 %copy-start = (bf16[1,256,1280]{2,1,0:T(8,128)(2,1)S(1)}, bf16[1,256,1280]{2,1,0:T(8,128)(2,1)}, u32[]{:S(2)}) copy-start(bf16[1,256,1280]{2,1,0:T(8,128)(2,1)} %param.9) | copy-start | bytes 1966084
  0.7 58.8 %slice-start.1 = ((s8[10485760]{0:T(1024)(128)(4,1)}), s8[4194304]{0:T(1024)(128)(4,1)S(1)}, s32[]{:S(2)}) async-start(s8[10485760]{0:T(1024)(128)(4,1)} %bitcast.7), calls=%async_computation.1 | async-start | bytes 8388608
  0.7 58.8 %slice-start.2 = ((s8[10485760]{0:T(1024)(128)(4,1)}), s8[2097152]{0:T(1024)(128)(4,1)S(1)}, s32[]{:S(2)}) async-start(s8[10485760]{0:T(1024)(128)(4,1)} %bitcast.7), calls=%async_computation.2 | async-start | bytes 4194304

commit v3 on v2

v3 whole, which is shorter than its diff:
```python
import functools

import jax
import jax.numpy as jnp
from jax import lax
from jax.experimental import pallas as pl
from jax.experimental.pallas import tpu as pltpu
from jax.sharding import PartitionSpec as P

HEAD = 128
BLOCK = 128
EPS = 1e-06
NEG = -1e30
LOG2E = 1.4426950408889634
MESH = pl.DeviceIdType.MESH
F32 = jnp.float32
BF16 = jnp.bfloat16


def remote(src, dst, sems, index, target):
    return pltpu.make_async_remote_copy(
        src_ref=src,
        dst_ref=dst,
        send_sem=sems[0].at[index],
        recv_sem=sems[1].at[index],
        device_id=target,
        device_id_type=MESH,
    )


class Layout:
    def __init__(self, cache_len, row_len, n_docs):
        self.n = n_docs
        self.c_len = [cache_len[0, d] for d in range(n_docs)]
        self.r_len = [row_len[0, d] for d in range(n_docs)]
        self.r_start, self.r_end = [], []
        total = jnp.int32(0)
        for length in self.r_len:
            self.r_start.append(total)
            total = total + length
            self.r_end.append(total)

    def _sum(self, tests, values):
        total = jnp.where(tests[0], values[0], 0)
        for test, value in zip(tests[1:], values[1:]):
            total = total + jnp.where(test, value, 0)
        return total

    def ranges(self, first, last):
        past = [end <= first for end in self.r_end]
        begun = [start <= last for start in self.r_start]
        return self._sum(past, self.c_len), self._sum(begun, self.c_len), self._sum(past, self.r_len)


def lane_rows(first):
    return first + lax.broadcasted_iota(jnp.int32, (1, BLOCK), 1)


def align_down(value):
    return lax.div(value, 16) * 16


def reset_state(m_s, l_s, acc_s):
    m_s[...] = jnp.full(m_s.shape, NEG, F32)
    l_s[...] = jnp.zeros(l_s.shape, F32)
    acc_s[...] = jnp.zeros(acc_s.shape, F32)


def attend_chunk(hist, start, size, low, high, queries, m_s, l_s, acc_s):
    scale = HEAD ** (-0.5) * LOG2E
    place0 = jnp.minimum(lax.div(start, 16), (hist.shape[0] - size) // 16) * 16
    at = pl.ds(place0, size)
    keys = hist[at, :HEAD]
    values_t = hist[at, HEAD:].T
    place = place0 + lax.broadcasted_iota(jnp.int32, (size, BLOCK), 0)
    bias = jnp.where((place >= jnp.maximum(low, start)) & (place < high), 0.0, 2 * NEG)
    bias = jnp.concatenate([bias, bias], axis=1)
    heads = len(queries)
    scores = []
    for h in range(0, heads, 2):
        pair = jnp.concatenate([queries[h], queries[h + 1]], axis=0)
        scores.append(
            lax.dot_general(keys, pair, (((1,), (1,)), ((), ())), preferred_element_type=F32)
        )
    weighted = []
    for i, score in enumerate(scores):
        cols = pl.ds(i * 2 * BLOCK, 2 * BLOCK)
        score = score + bias
        prior = m_s[:, cols]
        newest = jnp.maximum(prior, jnp.max(score, axis=0, keepdims=True))
        weights = jnp.exp2((score - newest) * scale)
        rescale = jnp.exp2((prior - newest) * scale)
        m_s[:, cols] = newest
        l_s[:, cols] = l_s[:, cols] * rescale + jnp.sum(weights, axis=0, keepdims=True)
        weighted.append((weights.astype(BF16), rescale))
    for i, (weights, rescale) in enumerate(weighted):
        cols = pl.ds(i * 2 * BLOCK, 2 * BLOCK)
        product = jnp.dot(values_t, weights, preferred_element_type=F32)
        acc_s[:, cols] = acc_s[:, cols] * rescale + product


def finish_block(heads, m_s, l_s, acc_s, store):
    for h in range(heads):
        cols = pl.ds(h * BLOCK, BLOCK)
        store(cols, (acc_s[:, cols] / l_s[:, cols]).T.astype(BF16))


CHUNK = 1024
EARLY = 4

def project_kernel(
    n_dp, n_t, n_docs, tok, gain_hbm, wq_hbm, wkv_hbm, cache, cache_len, row_len,
    q_out, cache_all, kv_all, m_s, l_s, acc_s,
    xs, gain, wq, wkv, normed, kv_own, w_sem, loc_sem,
    z_send, z_recv, y_send, y_recv, k_send, k_recv,
):
    rank = lax.axis_index("dp")
    t = lax.axis_index("tensor")
    right, left = lax.rem(t + 1, n_t), lax.rem(t + n_t - 1, n_t)
    over = lax.rem(t + 2, n_t)
    up, down = lax.rem(rank + 2, n_dp), lax.rem(rank + n_dp - 2, n_dp)
    across = lax.rem(rank + 4, n_dp)

    def twin_of(r):
        return r + 1 - 2 * lax.rem(r, 2)

    twin = twin_of(rank)
    z, y, k = (z_send, z_recv), (y_send, y_recv), (k_send, k_recv)
    half = BLOCK // 2
    span = cache.shape[0]
    mid = span // 2
    held = kv_own.shape[0]
    heads = q_out.shape[1]

    def cached_at(slot, lower, upper):
        return cache_all.at[pl.ds(pl.multiple_of(slot * span + lower, mid), upper - lower)]

    def fresh_at(slot, block):
        return kv_all.at[pl.ds(pl.multiple_of(slot * held + block * BLOCK, BLOCK), BLOCK)]

    w_copies = [
        pltpu.make_async_copy(wq_hbm, wq, w_sem.at[0]),
        pltpu.make_async_copy(wkv_hbm, wkv, w_sem.at[1]),
        pltpu.make_async_copy(gain_hbm, gain, w_sem.at[2]),
    ]
    own_tok = pltpu.make_async_copy(tok, xs.at[t], loc_sem.at[2])
    own_cache = pltpu.make_async_copy(cache, cached_at(rank, 0, span), loc_sem.at[0])

    barrier = pltpu.get_barrier_semaphore()
    for other in (left, right):
        pl.semaphore_signal(barrier, inc=1, device_id={"tensor": other}, device_id_type=MESH)
    for other in (up, down, across, twin):
        pl.semaphore_signal(barrier, inc=1, device_id={"dp": other}, device_id_type=MESH)
    own_tok.start()
    own_cache.start()
    for copy in w_copies:
        copy.start()
    pl.semaphore_wait(barrier, 6)

    started = []

    def go(copy):
        copy.start()
        started.append(copy)

    def rows(block, way, kind):
        low = block * BLOCK + (half if (way == 0) == (kind == 1) else 0)
        return pl.ds(low, half)

    def z_go(block, way, kind):
        part = rows(block, way, kind)
        target, source = (right, left) if way == 0 else (left, right)
        slot = source if kind == 2 else t
        src = xs.at[slot, part] if kind == 2 else tok.at[part]
        index = block * 6 + way * 3 + kind
        go(remote(src, xs.at[slot, part], z, index, {"tensor": target}))

    def z_take(block, way, kind):
        source = left if way == 0 else right
        slot = over if kind == 2 else source
        here = xs.at[slot, rows(block, way, kind)]
        index = block * 6 + way * 3 + kind
        remote(here, here, z, index, {"tensor": source}).wait_recv()

    def y_take(index, slot, lower, upper):
        part = cached_at(slot, lower, upper)
        remote(part, part, y, index, {"dp": twin}).wait_recv()

    def y_go(index, slot, lower, upper, target):
        part = cached_at(slot, lower, upper)
        go(remote(part, part, y, index, {"dp": target}))

    def k_start(block):
        part = kv_own.at[pl.ds(block * BLOCK, BLOCK)]
        for i, target in enumerate((up, down, across, twin)):
            go(remote(part, fresh_at(rank, block), k, block * 7 + i, {"dp": target}))

    def k_take(index, slot, block):
        here = fresh_at(slot, block)
        remote(here, here, k, index, {"dp": twin}).wait_recv()

    def k_pass_on(block):
        for i, slot in enumerate((down, up, across)):
            k_take(block * 7 + i, slot, block)
            here = fresh_at(slot, block)
            go(remote(here, here, k, block * 7 + 4 + i, {"dp": twin}))

    def k_finish(block):
        k_take(block * 7 + 3, twin, block)
        for i, slot in enumerate((down, up, across)):
            k_take(block * 7 + 4 + i, twin_of(slot), block)

    def project_block(block):
        def norm_rows(step, carry):
            low = pl.multiple_of(block * BLOCK + step * 16, 16)
            low_here = pl.multiple_of(step * 16, 16)
            parts = [xs[i, pl.ds(low, 16), :].astype(F32) for i in range(n_t)]
            total = jnp.sum(parts[0] * parts[0], axis=1, keepdims=True)
            for part in parts[1:]:
                total += jnp.sum(part * part, axis=1, keepdims=True)
            width = parts[0].shape[1]
            factor = lax.rsqrt(total / (width * n_t) + EPS)
            for i, part in enumerate(parts):
                cols = pl.ds(i * width, width)
                scaled = part * factor * gain[:, cols].astype(F32)
                normed[pl.ds(low_here, 16), cols] = scaled.astype(BF16)
            return carry

        if block == 0:
            w_copies[2].wait()
        lax.fori_loop(0, BLOCK // 16, norm_rows, 0)
        if block == 0:
            w_copies[1].wait()
        made = jnp.dot(normed[...], wkv[...], preferred_element_type=F32)
        kv_own[pl.ds(block * BLOCK, BLOCK), :] = made.astype(BF16)
        k_start(block)
        if block == 0:
            w_copies[0].wait()

        def query_tile(n, carry):
            cols = pl.ds(pl.multiple_of(n * 256, 256), 256)
            tile = jnp.dot(normed[...], wq[:, cols], preferred_element_type=F32).astype(BF16)
            q_out[block, 2 * n] = tile[:, :HEAD]
            q_out[block, 2 * n + 1] = tile[:, HEAD:]
            return carry

        lax.fori_loop(0, wq.shape[1] // 256, query_tile, 0)

    for way in range(2):
        z_go(0, way, 0)
    for way in range(2):
        z_go(0, way, 1)
    go(remote(cache, cached_at(rank, 0, span), y, 0, {"dp": up}))
    go(remote(cache, cached_at(rank, 0, span), y, 1, {"dp": down}))
    go(remote(cache, cached_at(rank, 0, span), y, 4, {"dp": twin}))
    reset_state(m_s, l_s, acc_s)
    layout = Layout(cache_len, row_len, n_docs)
    first = rank * held
    c_low, c_high, r_low = layout.ranges(first, first + BLOCK - 1)
    row = lane_rows(first)
    lane_low, lane_high, lane_r_low = layout.ranges(row, row)

    for way in range(2):
        z_take(0, way, 0)
        z_go(0, way, 2)
    for way in range(2):
        z_go(1, way, 0)
    for way in range(2):
        z_go(1, way, 1)
    own_tok.wait()
    for way in range(2):
        z_take(0, way, 1)
        z_take(0, way, 2)
    y_take(0, down, 0, span)
    y_go(2, down, 0, mid, up)
    y_go(5, down, 0, span, twin)
    y_take(1, up, 0, span)
    y_go(3, up, mid, span, down)
    y_go(6, up, 0, span, twin)
    project_block(0)
    for way in range(2):
        z_take(1, way, 0)
        z_go(1, way, 2)
    y_take(2, across, 0, mid)
    y_go(7, across, 0, mid, twin)
    y_take(3, across, mid, span)
    y_go(8, across, mid, span, twin)
    k_pass_on(0)
    own_cache.wait()
    y_take(4, twin, 0, span)
    y_take(5, twin_of(down), 0, span)
    y_take(6, twin_of(up), 0, span)
    y_take(7, twin_of(across), 0, mid)
    y_take(8, twin_of(across), mid, span)

    def early(c, carry):
        queries = [q_out[0, h] for h in range(heads)]
        start = align_down(c_low) + c * CHUNK
        attend_chunk(cache_all, start, CHUNK, lane_low, lane_high, queries, m_s, l_s, acc_s)
        return carry

    lax.fori_loop(0, EARLY // 2, early, 0)
    for way in range(2):
        z_take(1, way, 1)
        z_take(1, way, 2)
    project_block(1)
    own_kv = pltpu.make_async_copy(
        kv_own, kv_all.at[pl.ds(pl.multiple_of(rank * held, held), held)], loc_sem.at[1]
    )
    own_kv.start()
    k_pass_on(1)
    lax.fori_loop(EARLY // 2, EARLY, early, 0)
    for block in range(2):
        k_finish(block)
    own_kv.wait()
    for copy in started:
        copy.wait_send()


def project(own_rows, gain, w_query, w_kv, cache, cache_len, row_len, n_dp, n_t):
    rows, width = own_rows.shape
    blocks = rows // BLOCK
    full, heads_width = w_query.shape
    kv_width = w_kv.shape[1]
    heads = heads_width // HEAD
    span = cache.shape[0]
    vmem = pl.BlockSpec(memory_space=pltpu.VMEM)
    smem = pl.BlockSpec(memory_space=pltpu.SMEM)
    hbm = pl.BlockSpec(memory_space=pltpu.HBM)
    large = (own_rows, gain, w_query, w_kv, cache)
    return pl.pallas_call(
        functools.partial(project_kernel, n_dp, n_t, cache_len.shape[1]),
        out_shape=(
            jax.ShapeDtypeStruct((blocks, heads, BLOCK, HEAD), BF16),
            jax.ShapeDtypeStruct((n_dp * span, kv_width), BF16),
            jax.ShapeDtypeStruct((n_dp * rows, kv_width), BF16),
            jax.ShapeDtypeStruct((1, heads * BLOCK), F32),
            jax.ShapeDtypeStruct((1, heads * BLOCK), F32),
            jax.ShapeDtypeStruct((HEAD, heads * BLOCK), F32),
        ),
        in_specs=[hbm] * len(large) + [smem] * 2,
        out_specs=(vmem,) * 6,
        scratch_shapes=[
            pltpu.VMEM((n_t, rows, width), BF16),
            pltpu.VMEM(gain.shape, BF16),
            pltpu.VMEM((full, heads_width), BF16),
            pltpu.VMEM((full, kv_width), BF16),
            pltpu.VMEM((BLOCK, full), BF16),
            pltpu.VMEM((rows, kv_width), BF16),
            pltpu.SemaphoreType.DMA((3,)),
            pltpu.SemaphoreType.DMA((3,)),
            pltpu.SemaphoreType.DMA((12,)),
            pltpu.SemaphoreType.DMA((12,)),
            pltpu.SemaphoreType.DMA((9,)),
            pltpu.SemaphoreType.DMA((9,)),
            pltpu.SemaphoreType.DMA((14,)),
            pltpu.SemaphoreType.DMA((14,)),
        ],
        compiler_params=pltpu.CompilerParams(
            collective_id=0, has_side_effects=True, vmem_limit_bytes=40 * 1024 * 1024
        ),
        name="project",
    )(*(pltpu.with_memory_space_constraint(a, pltpu.HBM) for a in large + (cache_len, row_len)))


def attend_kernel(
    n_docs, cache_len, row_len, owner, q, cache, kv, m_in, l_in, acc_in, out, held, m_s, l_s, acc_s
):
    rank = lax.axis_index("dp")
    blocks, heads = q.shape[:2]
    layout = Layout(cache_len, row_len, n_docs)

    def one_block(block, carry):
        first = (rank * blocks + block) * BLOCK
        c_low, c_high, r_low = layout.ranges(first, first + BLOCK - 1)
        row = lane_rows(first)
        row_c_low, row_c_high, row_r_low = layout.ranges(row, row)
        queries = [q[block, h] for h in range(heads)]
        done = jnp.where(block == 0, EARLY, 0)

        @pl.when(block == 0)
        def _():
            m_s[...] = m_in[...]
            l_s[...] = l_in[...]
            acc_s[...] = acc_in[...]

        @pl.when(block > 0)
        def _():
            reset_state(m_s, l_s, acc_s)

        def one_range(source, low, high, lane_low, lane_high, done):
            begin = align_down(low)
            total = high - begin
            whole = total // CHUNK
            rest = total - whole * CHUNK

            def one(c, carry):
                start = begin + c * CHUNK
                attend_chunk(source, start, CHUNK, lane_low, lane_high, queries, m_s, l_s, acc_s)
                return carry

            lax.fori_loop(done, whole + (rest > CHUNK // 2).astype(jnp.int32), one, 0)

            @pl.when((rest > 0) & (rest <= CHUNK // 2) & (whole >= done))
            def _():
                start = begin + whole * CHUNK
                attend_chunk(
                    source, start, CHUNK // 2, lane_low, lane_high, queries, m_s, l_s, acc_s
                )

        one_range(cache, c_low, c_high, row_c_low, row_c_high, done)
        one_range(kv, r_low, first + BLOCK, row_r_low, row + 1, 0)

        def store(cols, value):
            out[pl.ds(pl.multiple_of(block * BLOCK, BLOCK), BLOCK), cols] = value

        finish_block(heads, m_s, l_s, acc_s, store)
        return carry

    lax.fori_loop(0, blocks, one_block, 0)

    def load_of(b, total):
        low = b * BLOCK
        work = low * BLOCK + (BLOCK * (BLOCK - 1)) // 2
        for d in range(n_docs):
            inside = jnp.minimum(layout.r_end[d], low + BLOCK) - jnp.maximum(layout.r_start[d], low)
            gain = layout.c_len[d] - layout.r_start[d] + 1
            work = work + jnp.maximum(inside, 0) * gain
        return total + jnp.where(owner[b] == rank, work, 0)

    total = lax.fori_loop(0, owner.shape[0], load_of, jnp.int32(0))
    held[0, 0] = total.astype(F32) * (2.0 / (BLOCK * (cache.shape[0] + kv.shape[0])))


def attend(cache_len, row_len, owner, q, cache, kv, state):
    blocks, heads = q.shape[:2]
    vmem = pl.BlockSpec(memory_space=pltpu.VMEM)
    smem = pl.BlockSpec(memory_space=pltpu.SMEM)
    return pl.pallas_call(
        functools.partial(attend_kernel, cache_len.shape[1]),
        out_shape=(
            jax.ShapeDtypeStruct((blocks * BLOCK, heads * HEAD), BF16),
            jax.ShapeDtypeStruct((1, 1), F32),
        ),
        in_specs=[smem] * 3 + [vmem] * 6,
        out_specs=(vmem, smem),
        scratch_shapes=[pltpu.VMEM(part.shape, F32) for part in state],
        compiler_params=pltpu.CompilerParams(vmem_limit_bytes=40 * 1024 * 1024),
        name="attend",
    )(cache_len, row_len, owner, q, cache, kv, *state)


PIECES = 4


def output_kernel(
    n_pipe, n_t, att, tok, wo, out,
    far, far_in, to_right, to_left, own, sent, from_left, from_right, section,
    z_send, z_recv, x_send, x_recv,
):
    s = lax.axis_index("pipe")
    t = lax.axis_index("tensor")
    right, left = lax.rem(t + 1, n_t), lax.rem(t + n_t - 1, n_t)
    over = lax.rem(t + 2, n_t)
    ahead, behind = lax.rem(s + 1, n_pipe), lax.rem(s + n_pipe - 1, n_pipe)
    z, x = (z_send, z_recv), (x_send, x_recv)
    width = tok.shape[1]
    size = tok.shape[0] // PIECES
    half = size // 2
    barrier = pltpu.get_barrier_semaphore()
    for other in (left, right):
        pl.semaphore_signal(barrier, inc=1, device_id={"tensor": other}, device_id_type=MESH)
    for other in (ahead, behind):
        pl.semaphore_signal(barrier, inc=1, device_id={"pipe": other}, device_id_type=MESH)
    pl.semaphore_wait(barrier, 4)

    def multiply(target, store):
        def tile(n, carry):
            cols = pl.ds(pl.multiple_of(n * 256, 256), 256)
            out_cols = pl.ds(pl.multiple_of(target * width + n * 256, 256), 256)
            store(cols, jnp.dot(att[...], wo[:, out_cols], preferred_element_type=F32))
            return carry

        lax.fori_loop(0, width // 256, tile, 0)

    started = []

    def go(copy):
        copy.start()
        started.append(copy)

    def span(p, way):
        return pl.ds(p * size + way * half, half)

    def far_copy(p, way):
        target = right if way == 0 else left
        return remote(far.at[span(p, way)], far_in.at[span(p, way)], z, p * 6 + way, {"tensor": target})

    def near_copy(p, way, kind):
        part = span(p, way if kind == 1 else 1 - way)
        target, box = (right, from_left) if way == 0 else (left, from_right)
        return remote(sent.at[way, part], box.at[part], z, p * 6 + 2 + 2 * kind + way, {"tensor": target})

    def store_far(cols, value):
        far[:, cols] = value.astype(BF16)

    multiply(over, store_far)
    for p in range(PIECES):
        for way in range(2):
            go(far_copy(p, way))

    def store_right(cols, value):
        to_right[:, cols] = value

    def store_left(cols, value):
        to_left[:, cols] = value

    multiply(right, store_right)
    multiply(left, store_left)
    held = (to_right, to_left)
    for p in range(PIECES):
        for way in range(2):
            part = span(p, 1 - way)
            sent[way, part, :] = held[way][part, :].astype(BF16)
            go(near_copy(p, way, 0))
        for way in range(2):
            part = span(p, way)
            far_copy(p, way).wait_recv()
            sent[way, part, :] = (held[way][part, :] + far_in[part, :].astype(F32)).astype(BF16)
            go(near_copy(p, way, 1))

    def store_own(cols, value):
        own[:, cols] = value + tok[:, cols].astype(F32)

    multiply(t, store_own)
    for p in range(PIECES):
        for way in range(2):
            near_copy(p, way, 0).wait_recv()
            near_copy(p, way, 1).wait_recv()
        part = pl.ds(p * size, size)
        total = from_left[part, :].astype(F32) + from_right[part, :].astype(F32)
        section[part, :] = (own[part, :] + total).astype(BF16)
        go(remote(section.at[part], out.at[part], x, p, {"pipe": ahead}))
    for p in range(PIECES):
        part = pl.ds(p * size, size)
        remote(section.at[part], out.at[part], x, p, {"pipe": ahead}).wait_recv()
    for copy in started:
        copy.wait_send()


def output(att, own_rows, w_out, n_pipe, n_t):
    rows, width = own_rows.shape
    vmem = pl.BlockSpec(memory_space=pltpu.VMEM)
    anywhere = pl.BlockSpec(memory_space=pl.ANY)
    whole = (rows, width)
    return pl.pallas_call(
        functools.partial(output_kernel, n_pipe, n_t),
        out_shape=jax.ShapeDtypeStruct(whole, BF16),
        in_specs=[vmem, vmem, vmem],
        out_specs=anywhere,
        scratch_shapes=[
            pltpu.VMEM(whole, BF16),
            pltpu.VMEM(whole, BF16),
            pltpu.VMEM(whole, F32),
            pltpu.VMEM(whole, F32),
            pltpu.VMEM(whole, F32),
            pltpu.VMEM((2,) + whole, BF16),
            pltpu.VMEM(whole, BF16),
            pltpu.VMEM(whole, BF16),
            pltpu.VMEM(whole, BF16),
            pltpu.SemaphoreType.DMA((6 * PIECES,)),
            pltpu.SemaphoreType.DMA((6 * PIECES,)),
            pltpu.SemaphoreType.DMA((PIECES,)),
            pltpu.SemaphoreType.DMA((PIECES,)),
        ],
        compiler_params=pltpu.CompilerParams(
            collective_id=1, has_side_effects=True, vmem_limit_bytes=40 * 1024 * 1024
        ),
        name="output",
    )(att, own_rows, w_out)


def on_device(
    tokens, norm_gain, w_query, key_value_weight, w_out, cache_kv,
    cache_lengths, row_lengths, block_owner,
):
    n_pipe, n_dp, n_t = (lax.axis_size(a) for a in ("pipe", "dp", "tensor"))
    own_rows = tokens[0]
    span = cache_kv.shape[1]
    cache = cache_kv.reshape(span, cache_kv.shape[3])
    q, cache_all, kv_all, *state = project(
        own_rows, norm_gain, w_query[0], key_value_weight[0], cache,
        cache_lengths, row_lengths, n_dp, n_t,
    )
    owner = block_owner.reshape(-1)
    att, held = attend(cache_lengths, row_lengths, owner, q, cache_all, kv_all, state)
    handed = output(att, own_rows, w_out[0], n_pipe, n_t)
    return handed[None], held


def solution(mesh):
    placed = (
        P("pipe", "dp", "tensor"),
        P("pipe", None),
        P("pipe", None, "tensor"),
        P("pipe", None, "tensor"),
        P("pipe", "tensor", None),
        P("pipe", "dp", "tensor", None),
        P("pipe", None),
        P("pipe", None),
        P("pipe", None, None),
    )
    return jax.shard_map(
        on_device,
        mesh=mesh,
        in_specs=placed,
        out_specs=(P("pipe", "dp", "tensor"), P("pipe", "dp")),
        check_vma=False,
    )
```

time: 95 us -> 92.9 us (0.978)
  the two profiles are of different devices: /device:TPU:8 before, /device:TPU:25 now
where the time goes in v3:
time: 92.9 us; the launch traced here: 92.8 us
  Pallas kernels  91.1 us (98%)
    pallas_call x1, Pallas kernels, project(): pl.pallas_call(functools.partial(project_kernel, n_dp, n_t, cache_len.sha...  43.4 us
    pallas_call x1, Pallas kernels, output(): pl.pallas_call(functools.partial(output_kernel, n_pipe, n_t), out_shape=j...  39.3 us
    pallas_call x1, Pallas kernels, attend(): pl.pallas_call(functools.partial(attend_kernel, cache_len.shape[1]), out_...  8.47 us

profile of v3, /device:TPU:25, one launch (start us, length us, event | category | flops | bytes accessed | tf_op | source)
XLA Modules:
  0.0 92.8 jit_solution(17127695099435643362)
XLA Ops:
  0.6 0.0 copy-start.2
  0.6 0.0 copy-start.1
  0.7 0.0 copy-start.3
  0.7 0.0 slice-start
  0.7 0.0 copy-start
  0.7 0.0 slice-start.1
  0.7 0.0 slice-start.2
  0.7 43.4 %project.1 = (bf16[2,8,128,128]{3,2,1,0:T(8,128)(2,1)S(1)}, bf16[8192,256]{1,0:T(8,128)(2,1)S(1)}, bf16[2048,256]{1,0:T(8,128)(2,1)S(1)}, f32[1,1024]{1,0:T(1,12...) custom-call(bf16[256,1280]{1,0:T(8,128)(2,1)} %bitcast.10, bf16[1,5120]{1,0:T(2,128)(2,1)} %gain_hbm.1, ...), custom_call_target="tpu_custom_call" | custom-call | tf_op jit(solution)/shard_map/project/pallas_call | solution.py:331
  44.1 0.0 copy-done.2
  44.1 0.0 copy-done.1
  44.1 0.0 copy-done.3
  44.1 8.5 %attend.1 = (bf16[256,1024]{1,0:T(8,128)(2,1)S(1)}, f32[1,1]{1,0:T(1,128)}) custom-call(s32[1,4]{1,0:T(1,128)S(1)} %copy-done.1, s32[1,4]{1,0:T(1,128)S(1)} %copy-done.2, s32[16]{0:T(128)S(1)} %bitcast.13, bf16[2,8,128,128]{3,2,1,0:T(8,128)(2,1)S(1)} %get-tuple-element.10.q, bf16[8192,256]{1,0:T(8,128)(2,1)S(1)} %get-tuple-element.11.cache, ...), custom_call_target="tpu_custom_call" | custom-call | tf_op jit(solution)/shard_map/attend/pallas_call | solution.py:439
  52.6 0.0 slice-done
  52.6 0.0 copy-done
  52.6 0.0 slice-done.1
  52.6 0.0 slice-done.2
  52.6 39.3 %output.1 = bf16[256,1280]{1,0:T(8,128)(2,1)S(1)} custom-call(bf16[256,1024]{1,0:T(8,128)(2,1)S(1)} %get-tuple-element.16.att, bf16[256,1280]{1,0:T(8,128)(2,1)S(1)} %bitcast.11, bf16[1024,5120]{1,0:T(8,128)(2,1)S(1)} %bitcast.9), custom_call_target="tpu_custom_call" | custom-call | tf_op jit(solution)/shard_map/output/pallas_call | solution.py:556
  91.9 0.8 copy.12
  (1 shorter events, 0.0 us)
Async XLA Ops:
  0.6 43.4 %copy-start.2 = (s32[1,4]{1,0:T(1,128)S(1)}, s32[1,4]{1,0:T(1,128)}, u32[]{:S(2)}) copy-start(s32[1,4]{1,0:T(1,128)} %row_len.3) | copy-start | bytes 52
  0.6 43.4 %copy-start.1 = (s32[1,4]{1,0:T(1,128)S(1)}, s32[1,4]{1,0:T(1,128)}, u32[]{:S(2)}) copy-start(s32[1,4]{1,0:T(1,128)} %cache_len.3) | copy-start | bytes 52
  0.7 43.4 %copy-start.3 = (s32[1,16,1]{1,2,0:T(1,128)S(1)}, s32[1,16,1]{1,2,0:T(1,128)}, u32[]{:S(2)}) copy-start(s32[1,16,1]{1,2,0:T(1,128)} %param.17) | copy-start | bytes 196
  0.7 51.9 %slice-start = ((s8[10485760]{0:T(1024)(128)(4,1)}), s8[4194304]{0:T(1024)(128)(4,1)S(1)}, s32[]{:S(2)}) async-start(s8[10485760]{0:T(1024)(128)(4,1)} %bitcast.7), calls=%async_computation | async-start | bytes 8388608
  0.7 51.9 %copy-start = (bf16[1,256,1280]{2,1,0:T(8,128)(2,1)S(1)}, bf16[1,256,1280]{2,1,0:T(8,128)(2,1)}, u32[]{:S(2)}) copy-start(bf16[1,256,1280]{2,1,0:T(8,128)(2,1)} %param.9) | copy-start | bytes 1966084
  0.7 51.9 %slice-start.1 = ((s8[10485760]{0:T(1024)(128)(4,1)}), s8[4194304]{0:T(1024)(128)(4,1)S(1)}, s32[]{:S(2)}) async-start(s8[10485760]{0:T(1024)(128)(4,1)} %bitcast.7), calls=%async_computation.1 | async-start | bytes 8388608
  0.7 51.9 %slice-start.2 = ((s8[10485760]{0:T(1024)(128)(4,1)}), s8[2097152]{0:T(1024)(128)(4,1)S(1)}, s32[]{:S(2)}) async-start(s8[10485760]{0:T(1024)(128)(4,1)} %bitcast.7), calls=%async_computation.2 | async-start | bytes 4194304

commit v4 on v3

--- a/solution.py
+++ b/solution.py
@@ -99,14 +99,15 @@
         acc_s[:, cols] = acc_s[:, cols] * rescale + product
 
 
-def finish_block(heads, m_s, l_s, acc_s, store):
+def finish_block(heads, out, m_s, l_s, acc_s):
     for h in range(heads):
         cols = pl.ds(h * BLOCK, BLOCK)
-        store(cols, (acc_s[:, cols] / l_s[:, cols]).T.astype(BF16))
+        out[:, cols] = (acc_s[:, cols] / l_s[:, cols]).T.astype(BF16)
 
 
 CHUNK = 1024
 EARLY = 4
+LATE = 4
 
 def project_kernel(
     n_dp, n_t, n_docs, tok, gain_hbm, wq_hbm, wkv_hbm, cache, cache_len, row_len,
@@ -114,6 +115,7 @@
     xs, gain, wq, wkv, normed, kv_own, w_sem, loc_sem,
     z_send, z_recv, y_send, y_recv, k_send, k_recv,
 ):
+    s = lax.axis_index("pipe")
     rank = lax.axis_index("dp")
     t = lax.axis_index("tensor")
     right, left = lax.rem(t + 1, n_t), lax.rem(t + n_t - 1, n_t)
@@ -148,9 +150,9 @@
 
     barrier = pltpu.get_barrier_semaphore()
     for other in (left, right):
-        pl.semaphore_signal(barrier, inc=1, device_id={"tensor": other}, device_id_type=MESH)
+        pl.semaphore_signal(barrier, inc=1, device_id=(s, rank, other), device_id_type=MESH)
     for other in (up, down, across, twin):
-        pl.semaphore_signal(barrier, inc=1, device_id={"dp": other}, device_id_type=MESH)
+        pl.semaphore_signal(barrier, inc=1, device_id=(s, other, t), device_id_type=MESH)
     own_tok.start()
     own_cache.start()
     for copy in w_copies:
@@ -173,37 +175,37 @@
         slot = source if kind == 2 else t
         src = xs.at[slot, part] if kind == 2 else tok.at[part]
         index = block * 6 + way * 3 + kind
-        go(remote(src, xs.at[slot, part], z, index, {"tensor": target}))
+        go(remote(src, xs.at[slot, part], z, index, (s, rank, target)))
 
     def z_take(block, way, kind):
         source = left if way == 0 else right
         slot = over if kind == 2 else source
         here = xs.at[slot, rows(block, way, kind)]
         index = block * 6 + way * 3 + kind
-        remote(here, here, z, index, {"tensor": source}).wait_recv()
+        remote(here, here, z, index, (s, rank, source)).wait_recv()
 
     def y_take(index, slot, lower, upper):
         part = cached_at(slot, lower, upper)
-        remote(part, part, y, index, {"dp": twin}).wait_recv()
+        remote(part, part, y, index, (s, twin, t)).wait_recv()
 
     def y_go(index, slot, lower, upper, target):
         part = cached_at(slot, lower, upper)
-        go(remote(part, part, y, index, {"dp": target}))
+        go(remote(part, part, y, index, (s, target, t)))
 
     def k_start(block):
         part = kv_own.at[pl.ds(block * BLOCK, BLOCK)]
         for i, target in enumerate((up, down, across, twin)):
-            go(remote(part, fresh_at(rank, block), k, block * 7 + i, {"dp": target}))
+            go(remote(part, fresh_at(rank, block), k, block * 7 + i, (s, target, t)))
 
     def k_take(index, slot, block):
         here = fresh_at(slot, block)
-        remote(here, here, k, index, {"dp": twin}).wait_recv()
+        remote(here, here, k, index, (s, twin, t)).wait_recv()
 
     def k_pass_on(block):
         for i, slot in enumerate((down, up, across)):
             k_take(block * 7 + i, slot, block)
             here = fresh_at(slot, block)
-            go(remote(here, here, k, block * 7 + 4 + i, {"dp": twin}))
+            go(remote(here, here, k, block * 7 + 4 + i, (s, twin, t)))
 
     def k_finish(block):
         k_take(block * 7 + 3, twin, block)
@@ -250,9 +252,9 @@
         z_go(0, way, 0)
     for way in range(2):
         z_go(0, way, 1)
-    go(remote(cache, cached_at(rank, 0, span), y, 0, {"dp": up}))
-    go(remote(cache, cached_at(rank, 0, span), y, 1, {"dp": down}))
-    go(remote(cache, cached_at(rank, 0, span), y, 4, {"dp": twin}))
+    go(remote(cache, cached_at(rank, 0, span), y, 0, (s, up, t)))
+    go(remote(cache, cached_at(rank, 0, span), y, 1, (s, down, t)))
+    go(remote(cache, cached_at(rank, 0, span), y, 4, (s, twin, t)))
     reset_state(m_s, l_s, acc_s)
     layout = Layout(cache_len, row_len, n_docs)
     first = rank * held
@@ -308,8 +310,9 @@
         kv_own, kv_all.at[pl.ds(pl.multiple_of(rank * held, held), held)], loc_sem.at[1]
     )
     own_kv.start()
+    lax.fori_loop(EARLY // 2, EARLY - 1, early, 0)
     k_pass_on(1)
-    lax.fori_loop(EARLY // 2, EARLY, early, 0)
+    lax.fori_loop(EARLY - 1, EARLY, early, 0)
     for block in range(2):
         k_finish(block)
     own_kv.wait()
@@ -357,14 +360,15 @@
             pltpu.SemaphoreType.DMA((14,)),
         ],
         compiler_params=pltpu.CompilerParams(
-            collective_id=0, has_side_effects=True, vmem_limit_bytes=40 * 1024 * 1024
+            collective_id=0, has_side_effects=True, vmem_limit_bytes=32 * 1024 * 1024
         ),
         name="project",
     )(*(pltpu.with_memory_space_constraint(a, pltpu.HBM) for a in large + (cache_len, row_len)))
 
 
 def attend_kernel(
-    n_docs, cache_len, row_len, owner, q, cache, kv, m_in, l_in, acc_in, out, held, m_s, l_s, acc_s
+    n_docs, cache_len, row_len, owner, q, cache, kv, m_in, l_in, acc_in,
+    out, held, m_s, l_s, acc_s,
 ):
     rank = lax.axis_index("dp")
     blocks, heads = q.shape[:2]
@@ -376,7 +380,6 @@
         row = lane_rows(first)
         row_c_low, row_c_high, row_r_low = layout.ranges(row, row)
         queries = [q[block, h] for h in range(heads)]
-        done = jnp.where(block == 0, EARLY, 0)
 
         @pl.when(block == 0)
         def _():
@@ -408,13 +411,14 @@
                     source, start, CHUNK // 2, lane_low, lane_high, queries, m_s, l_s, acc_s
                 )
 
+        done = jnp.where(block == 0, EARLY, LATE)
         one_range(cache, c_low, c_high, row_c_low, row_c_high, done)
-        one_range(kv, r_low, first + BLOCK, row_r_low, row + 1, 0)
-
-        def store(cols, value):
-            out[pl.ds(pl.multiple_of(block * BLOCK, BLOCK), BLOCK), cols] = value
-
-        finish_block(heads, m_s, l_s, acc_s, store)
+
+        @pl.when(block == 0)
+        def _():
+            one_range(kv, r_low, first + BLOCK, row_r_low, row + 1, 0)
+            finish_block(heads, out, m_s, l_s, acc_s)
+
         return carry
 
     lax.fori_loop(0, blocks, one_block, 0)
@@ -439,42 +443,44 @@
     return pl.pallas_call(
         functools.partial(attend_kernel, cache_len.shape[1]),
         out_shape=(
-            jax.ShapeDtypeStruct((blocks * BLOCK, heads * HEAD), BF16),
+            jax.ShapeDtypeStruct((BLOCK, heads * HEAD), BF16),
             jax.ShapeDtypeStruct((1, 1), F32),
-        ),
+        )
+        + tuple(jax.ShapeDtypeStruct(part.shape, F32) for part in state),
         in_specs=[smem] * 3 + [vmem] * 6,
-        out_specs=(vmem, smem),
-        scratch_shapes=[pltpu.VMEM(part.shape, F32) for part in state],
-        compiler_params=pltpu.CompilerParams(vmem_limit_bytes=40 * 1024 * 1024),
+        out_specs=(vmem, smem) + (vmem,) * 3,
+        compiler_params=pltpu.CompilerParams(vmem_limit_bytes=32 * 1024 * 1024),
         name="attend",
     )(cache_len, row_len, owner, q, cache, kv, *state)
 
 
-PIECES = 4
+PIECES = 2
 
 
 def output_kernel(
-    n_pipe, n_t, att, tok, wo, out,
-    far, far_in, to_right, to_left, own, sent, from_left, from_right, section,
+    n_pipe, n_t, n_docs, cache_len, row_len, att0, tok, wo, q, cache, kv, m_in, l_in, acc_in, out,
+    m_s, l_s, acc_s, att1, far, far_in, to_right, to_left, own, sent, from_left, from_right, section,
     z_send, z_recv, x_send, x_recv,
 ):
     s = lax.axis_index("pipe")
+    rank = lax.axis_index("dp")
     t = lax.axis_index("tensor")
     right, left = lax.rem(t + 1, n_t), lax.rem(t + n_t - 1, n_t)
     over = lax.rem(t + 2, n_t)
     ahead, behind = lax.rem(s + 1, n_pipe), lax.rem(s + n_pipe - 1, n_pipe)
     z, x = (z_send, z_recv), (x_send, x_recv)
     width = tok.shape[1]
-    size = tok.shape[0] // PIECES
+    size = BLOCK // PIECES
     half = size // 2
+    blocks, heads = q.shape[:2]
+
     barrier = pltpu.get_barrier_semaphore()
     for other in (left, right):
-        pl.semaphore_signal(barrier, inc=1, device_id={"tensor": other}, device_id_type=MESH)
+        pl.semaphore_signal(barrier, inc=1, device_id=(s, rank, other), device_id_type=MESH)
     for other in (ahead, behind):
-        pl.semaphore_signal(barrier, inc=1, device_id={"pipe": other}, device_id_type=MESH)
-    pl.semaphore_wait(barrier, 4)
-
-    def multiply(target, store):
+        pl.semaphore_signal(barrier, inc=1, device_id=(other, rank, t), device_id_type=MESH)
+
+    def multiply(att, target, store):
         def tile(n, carry):
             cols = pl.ds(pl.multiple_of(n * 256, 256), 256)
             out_cols = pl.ds(pl.multiple_of(target * width + n * 256, 256), 256)
@@ -492,92 +498,165 @@
     def span(p, way):
         return pl.ds(p * size + way * half, half)
 
+    def local(p, way):
+        return pl.ds(p % PIECES * size + way * half, half)
+
     def far_copy(p, way):
         target = right if way == 0 else left
-        return remote(far.at[span(p, way)], far_in.at[span(p, way)], z, p * 6 + way, {"tensor": target})
+        part = span(p, way)
+        return remote(far.at[part], far_in.at[part], z, p * 6 + way, (s, rank, target))
 
     def near_copy(p, way, kind):
         part = span(p, way if kind == 1 else 1 - way)
         target, box = (right, from_left) if way == 0 else (left, from_right)
-        return remote(sent.at[way, part], box.at[part], z, p * 6 + 2 + 2 * kind + way, {"tensor": target})
-
-    def store_far(cols, value):
-        far[:, cols] = value.astype(BF16)
-
-    multiply(over, store_far)
-    for p in range(PIECES):
+        index = p * 6 + 2 + 2 * kind + way
+        return remote(sent.at[way, part], box.at[part], z, index, (s, rank, target))
+
+    held = (to_right, to_left)
+
+    def pieces(block):
+        return range(block * PIECES, block * PIECES + PIECES)
+
+    def block_rows(block):
+        return pl.ds(block * BLOCK, BLOCK)
+
+    def multiply_far(block, att):
+        def store_far(cols, value):
+            far[block_rows(block), cols] = value.astype(BF16)
+
+        multiply(att, over, store_far)
+
+    def send_far(block):
+        for p in pieces(block):
+            for way in range(2):
+                go(far_copy(p, way))
+
+    def multiply_near(block, att):
+        def store_right(cols, value):
+            to_right[:, cols] = value
+
+        def store_left(cols, value):
+            to_left[:, cols] = value
+
+        multiply(att, right, store_right)
+        multiply(att, left, store_left)
+
+    def multiply_own(block, att):
+        def store_own(cols, value):
+            own[:, cols] = value + tok[block_rows(block), cols].astype(F32)
+
+        multiply(att, t, store_own)
+
+    def send_free(p):
         for way in range(2):
-            go(far_copy(p, way))
-
-    def store_right(cols, value):
-        to_right[:, cols] = value
-
-    def store_left(cols, value):
-        to_left[:, cols] = value
-
-    multiply(right, store_right)
-    multiply(left, store_left)
-    held = (to_right, to_left)
-    for p in range(PIECES):
-        for way in range(2):
-            part = span(p, 1 - way)
-            sent[way, part, :] = held[way][part, :].astype(BF16)
+            sent[way, span(p, 1 - way), :] = held[way][local(p, 1 - way), :].astype(BF16)
             go(near_copy(p, way, 0))
+
+    def send_merged(p):
         for way in range(2):
             part = span(p, way)
             far_copy(p, way).wait_recv()
-            sent[way, part, :] = (held[way][part, :] + far_in[part, :].astype(F32)).astype(BF16)
+            both = held[way][local(p, way), :] + far_in[part, :].astype(F32)
+            sent[way, part, :] = both.astype(BF16)
             go(near_copy(p, way, 1))
 
-    def store_own(cols, value):
-        own[:, cols] = value + tok[:, cols].astype(F32)
-
-    multiply(t, store_own)
-    for p in range(PIECES):
+    def finish(p):
         for way in range(2):
             near_copy(p, way, 0).wait_recv()
             near_copy(p, way, 1).wait_recv()
         part = pl.ds(p * size, size)
         total = from_left[part, :].astype(F32) + from_right[part, :].astype(F32)
-        section[part, :] = (own[part, :] + total).astype(BF16)
-        go(remote(section.at[part], out.at[part], x, p, {"pipe": ahead}))
-    for p in range(PIECES):
+        mine = own[pl.ds(p % PIECES * size, size), :]
+        section[part, :] = (mine + total).astype(BF16)
+        go(remote(section.at[part], out.at[part], x, p, (ahead, rank, t)))
+
+    first = (rank * blocks + 1) * BLOCK
+    layout = Layout(cache_len, row_len, n_docs)
+    c_low, c_high, r_low = layout.ranges(first, first + BLOCK - 1)
+    row = lane_rows(first)
+    row_c_low, row_c_high, row_r_low = layout.ranges(row, row)
+
+    def cached(c, carry):
+        queries = [q[1, h] for h in range(heads)]
+        start = align_down(c_low) + c * CHUNK
+        attend_chunk(cache, start, CHUNK, row_c_low, row_c_high, queries, m_s, l_s, acc_s)
+        return carry
+
+    def fresh(start, amount):
+        queries = [q[1, h] for h in range(heads)]
+        attend_chunk(kv, start, amount, row_r_low, row + 1, queries, m_s, l_s, acc_s)
+
+    multiply_far(0, att0)
+    pl.semaphore_wait(barrier, 4)
+    send_far(0)
+    multiply_near(0, att0)
+    for p in pieces(0):
+        send_free(p)
+    multiply_own(0, att0)
+    m_s[...] = m_in[...]
+    l_s[...] = l_in[...]
+    acc_s[...] = acc_in[...]
+    lax.fori_loop(0, 1, cached, 0)
+    for p in pieces(0):
+        send_merged(p)
+    lax.fori_loop(1, LATE, cached, 0)
+    finish(0)
+    begin = align_down(r_low)
+    fresh(begin, CHUNK)
+    fresh(begin + CHUNK, 2 * BLOCK)
+    finish_block(heads, att1, m_s, l_s, acc_s)
+    multiply_far(1, att1)
+    send_far(1)
+    for p in pieces(0):
+        if p > 0:
+            finish(p)
+    multiply_near(1, att1)
+    for p in pieces(1):
+        send_free(p)
+        send_merged(p)
+    multiply_own(1, att1)
+    for p in pieces(1):
+        finish(p)
+    for p in range(blocks * PIECES):
         part = pl.ds(p * size, size)
-        remote(section.at[part], out.at[part], x, p, {"pipe": ahead}).wait_recv()
+        remote(section.at[part], out.at[part], x, p, (ahead, rank, t)).wait_recv()
     for copy in started:
         copy.wait_send()
 
 
-def output(att, own_rows, w_out, n_pipe, n_t):
+def output(cache_len, row_len, att, own_rows, w_out, q, cache, kv, state, n_pipe, n_t):
     rows, width = own_rows.shape
+    copies = rows // BLOCK * PIECES
     vmem = pl.BlockSpec(memory_space=pltpu.VMEM)
-    anywhere = pl.BlockSpec(memory_space=pl.ANY)
-    whole = (rows, width)
+    smem = pl.BlockSpec(memory_space=pltpu.SMEM)
+    whole, one = (rows, width), (BLOCK, width)
     return pl.pallas_call(
-        functools.partial(output_kernel, n_pipe, n_t),
+        functools.partial(output_kernel, n_pipe, n_t, cache_len.shape[1]),
         out_shape=jax.ShapeDtypeStruct(whole, BF16),
-        in_specs=[vmem, vmem, vmem],
-        out_specs=anywhere,
-        scratch_shapes=[
+        in_specs=[smem] * 2 + [vmem] * 9,
+        out_specs=pl.BlockSpec(memory_space=pl.ANY),
+        scratch_shapes=[pltpu.VMEM(part.shape, F32) for part in state]
+        + [
+            pltpu.VMEM(att.shape, BF16),
             pltpu.VMEM(whole, BF16),
             pltpu.VMEM(whole, BF16),
-            pltpu.VMEM(whole, F32),
-            pltpu.VMEM(whole, F32),
-            pltpu.VMEM(whole, F32),
+            pltpu.VMEM(one, F32),
+            pltpu.VMEM(one, F32),
+            pltpu.VMEM(one, F32),
             pltpu.VMEM((2,) + whole, BF16),
             pltpu.VMEM(whole, BF16),
             pltpu.VMEM(whole, BF16),
             pltpu.VMEM(whole, BF16),
-            pltpu.SemaphoreType.DMA((6 * PIECES,)),
-            pltpu.SemaphoreType.DMA((6 * PIECES,)),
-            pltpu.SemaphoreType.DMA((PIECES,)),
-            pltpu.SemaphoreType.DMA((PIECES,)),
+            pltpu.SemaphoreType.DMA((6 * copies,)),
+            pltpu.SemaphoreType.DMA((6 * copies,)),
+            pltpu.SemaphoreType.DMA((copies,)),
+            pltpu.SemaphoreType.DMA((copies,)),
         ],
         compiler_params=pltpu.CompilerParams(
-            collective_id=1, has_side_effects=True, vmem_limit_bytes=40 * 1024 * 1024
+            collective_id=1, has_side_effects=True, vmem_limit_bytes=32 * 1024 * 1024
         ),
         name="output",
-    )(att, own_rows, w_out)
+    )(cache_len, row_len, att, own_rows, w_out, q, cache, kv, *state)
 
 
 def on_device(
@@ -593,8 +672,12 @@
         cache_lengths, row_lengths, n_dp, n_t,
     )
     owner = block_owner.reshape(-1)
-    att, held = attend(cache_lengths, row_lengths, owner, q, cache_all, kv_all, state)
-    handed = output(att, own_rows, w_out[0], n_pipe, n_t)
+    att, held, *state = attend(
+        cache_lengths, row_lengths, owner, q, cache_all, kv_all, state
+    )
+    handed = output(
+        cache_lengths, row_lengths, att, own_rows, w_out[0], q, cache_all, kv_all, state, n_pipe, n_t
+    )
     return handed[None], held
 
 

time: 92.9 us -> 87.9 us (0.946)
  the two profiles are of different devices: /device:TPU:25 before, /device:TPU:8 now
where the time goes in v4:
time: 87.9 us; the launch traced here: 87.2 us
  Pallas kernels  85.6 us (97%)
    pallas_call x1, Pallas kernels, project(): pl.pallas_call(functools.partial(project_kernel, n_dp, n_t, cache_len.sha...  42.2 us
    pallas_call x1, Pallas kernels, output(): pl.pallas_call(functools.partial(output_kernel, n_pipe, n_t, cache_len.sh...  40.3 us
    pallas_call x1, Pallas kernels, attend(): pl.pallas_call(functools.partial(attend_kernel, cache_len.shape[1]), out_...  3.07 us

profile of v4, /device:TPU:8, one launch (start us, length us, event | category | flops | bytes accessed | tf_op | source)
XLA Modules:
  0.0 87.2 jit_solution(915386778287087363)
XLA Ops:
  0.6 0.0 copy-start.2
  0.6 0.0 copy-start.1
  0.7 0.0 copy-start.3
  0.7 0.0 slice-start
  0.7 0.0 copy-start
  0.7 0.0 slice-start.1
  0.7 0.0 slice-start.2
  0.7 42.2 %project.1 = (bf16[2,8,128,128]{3,2,1,0:T(8,128)(2,1)S(1)}, bf16[8192,256]{1,0:T(8,128)(2,1)S(1)}, bf16[2048,256]{1,0:T(8,128)(2,1)S(1)}, f32[1,1024]{1,0:T(1,12...) custom-call(bf16[256,1280]{1,0:T(8,128)(2,1)} %bitcast.10, bf16[1,5120]{1,0:T(2,128)(2,1)} %gain_hbm.1, ...), custom_call_target="tpu_custom_call" | custom-call | tf_op jit(solution)/shard_map/project/pallas_call | solution.py:334
  42.9 0.0 copy-done.2
  42.9 0.0 copy-done.1
  42.9 0.0 copy-done.3
  42.9 3.1 %attend.1 = (bf16[128,1024]{1,0:T(8,128)(2,1)S(1)}, f32[1,1]{1,0:T(1,128)}, f32[1,1024]{1,0:T(1,128)S(1)}, f32[1,1024]{1,0:T(1,128)S(1)}, f32[128,1024]{1,0:T(8,128)S(1)}) custom-call(s32[1,4]{1,0:T(1,128)S(1)} %copy-done.1, s32[1,4]{1,0:T(1,128)S(1)} %copy-done.2, s32[16]{0:T(128)S(1)} %bitcast.13, bf16[2,8,128,128]{3,2,1,0:T(8,128)(2,1)S(1)} %get-tuple-element.13.q, ...), custom_call_target="tpu_custom_call" | custom-call | tf_op jit(solution)/shard_map/attend/pallas_call | solution.py:443
  46.0 0.0 slice-done
  46.0 0.0 copy-done
  46.0 0.0 slice-done.1
  46.0 0.0 slice-done.2
  46.0 40.3 %output.1 = bf16[256,1280]{1,0:T(8,128)(2,1)S(1)} custom-call(s32[1,4]{1,0:T(1,128)S(1)} %copy-done.1, s32[1,4]{1,0:T(1,128)S(1)} %copy-done.2, bf16[128,1024]{1,0:T(8,128)(2,1)S(1)} %get-tuple-element.19.att0, bf16[256,1280]{1,0:T(8,128)(2,1)S(1)} %bitcast.11, bf16[1024,5120]{1,0:T(8,128)(2,1)S(1)} %bitcast.9, ...), custom_call_target="tpu_custom_call" | custom-call | tf_op jit(solution)/shard_map/output/pallas_call | solution.py:633
  86.4 0.8 copy.12
  (1 shorter events, 0.0 us)
Async XLA Ops:
  0.6 42.2 %copy-start.2 = (s32[1,4]{1,0:T(1,128)S(1)}, s32[1,4]{1,0:T(1,128)}, u32[]{:S(2)}) copy-start(s32[1,4]{1,0:T(1,128)} %row_len.5) | copy-start | bytes 52
  0.6 42.2 %copy-start.1 = (s32[1,4]{1,0:T(1,128)S(1)}, s32[1,4]{1,0:T(1,128)}, u32[]{:S(2)}) copy-start(s32[1,4]{1,0:T(1,128)} %cache_len.5) | copy-start | bytes 52
  0.7 42.2 %copy-start.3 = (s32[1,16,1]{1,2,0:T(1,128)S(1)}, s32[1,16,1]{1,2,0:T(1,128)}, u32[]{:S(2)}) copy-start(s32[1,16,1]{1,2,0:T(1,128)} %param.17) | copy-start | bytes 196
  0.7 45.3 %slice-start = ((s8[10485760]{0:T(1024)(128)(4,1)}), s8[4194304]{0:T(1024)(128)(4,1)S(1)}, s32[]{:S(2)}) async-start(s8[10485760]{0:T(1024)(128)(4,1)} %bitcast.7), calls=%async_computation | async-start | bytes 8388608
  0.7 45.3 %copy-start = (bf16[1,256,1280]{2,1,0:T(8,128)(2,1)S(1)}, bf16[1,256,1280]{2,1,0:T(8,128)(2,1)}, u32[]{:S(2)}) copy-start(bf16[1,256,1280]{2,1,0:T(8,128)(2,1)} %param.9) | copy-start | bytes 1966084
  0.7 45.3 %slice-start.1 = ((s8[10485760]{0:T(1024)(128)(4,1)}), s8[4194304]{0:T(1024)(128)(4,1)S(1)}, s32[]{:S(2)}) async-start(s8[10485760]{0:T(1024)(128)(4,1)} %bitcast.7), calls=%async_computation.1 | async-start | bytes 8388608
  0.7 45.3 %slice-start.2 = ((s8[10485760]{0:T(1024)(128)(4,1)}), s8[2097152]{0:T(1024)(128)(4,1)S(1)}, s32[]{:S(2)}) async-start(s8[10485760]{0:T(1024)(128)(4,1)} %bitcast.7), calls=%async_computation.2 | async-start | bytes 4194304

commit v5 on v4

--- a/solution.py
+++ b/solution.py
@@ -287,7 +287,6 @@
     y_go(7, across, 0, mid, twin)
     y_take(3, across, mid, span)
     y_go(8, across, mid, span, twin)
-    k_pass_on(0)
     own_cache.wait()
     y_take(4, twin, 0, span)
     y_take(5, twin_of(down), 0, span)
@@ -311,6 +310,7 @@
     )
     own_kv.start()
     lax.fori_loop(EARLY // 2, EARLY - 1, early, 0)
+    k_pass_on(0)
     k_pass_on(1)
     lax.fori_loop(EARLY - 1, EARLY, early, 0)
     for block in range(2):
@@ -404,12 +404,14 @@
 
             lax.fori_loop(done, whole + (rest > CHUNK // 2).astype(jnp.int32), one, 0)
 
-            @pl.when((rest > 0) & (rest <= CHUNK // 2) & (whole >= done))
-            def _():
-                start = begin + whole * CHUNK
-                attend_chunk(
-                    source, start, CHUNK // 2, lane_low, lane_high, queries, m_s, l_s, acc_s
-                )
+            start = begin + whole * CHUNK
+
+            def remainder(size):
+                attend_chunk(source, start, size, lane_low, lane_high, queries, m_s, l_s, acc_s)
+
+            left = (rest <= CHUNK // 2) & (whole >= done)
+            pl.when(left & (rest > BLOCK))(lambda: remainder(CHUNK // 2))
+            pl.when(left & (rest > 0) & (rest <= BLOCK))(lambda: remainder(BLOCK))
 
         done = jnp.where(block == 0, EARLY, LATE)
         one_range(cache, c_low, c_high, row_c_low, row_c_high, done)
@@ -454,7 +456,7 @@
     )(cache_len, row_len, owner, q, cache, kv, *state)
 
 
-PIECES = 2
+PIECES = 4
 
 
 def output_kernel(

time: 87.9 us -> 85.8 us (0.976)
  Pallas kernels: 85.6 us -> 84 us
    pallas_call x1, Pallas kernels: 3.07 us -> 8.5 us  [attend(): pl.pallas_call(functools.partial(attend_kernel, cache_len.shape[1]), out_...]
    pallas_call x1, Pallas kernels: 40.3 us -> 34.9 us  [output(): pl.pallas_call(functools.partial(output_kernel, n_pipe, n_t, cache_len.sh...]
    pallas_call x1, Pallas kernels: 42.2 us -> 40.6 us  [project(): pl.pallas_call(functools.partial(project_kernel, n_dp, n_t, cache_len.sha...]
where the time goes in v5:
time: 85.8 us; the launch traced here: 85.7 us
  Pallas kernels  84 us (98%)
  local copies, waits for them, and re-layouts  0.87 us (1%)
    pallas_call x1, Pallas kernels, project(): pl.pallas_call(functools.partial(project_kernel, n_dp, n_t, cache_len.sha...  40.6 us
    pallas_call x1, Pallas kernels, output(): pl.pallas_call(functools.partial(output_kernel, n_pipe, n_t, cache_len.sh...  34.9 us
    pallas_call x1, Pallas kernels, attend(): pl.pallas_call(functools.partial(attend_kernel, cache_len.shape[1]), out_...  8.5 us

profile of v5, /device:TPU:8, one launch (start us, length us, event | category | flops | bytes accessed | tf_op | source)
XLA Modules:
  0.0 85.7 jit_solution(6174464633235606528)
XLA Ops:
  0.6 0.0 copy-start.2
  0.6 0.0 copy-start.1
  0.7 0.0 copy-start.3
  0.7 0.0 slice-start
  0.7 0.0 copy-start
  0.7 0.0 slice-start.1
  0.7 0.0 slice-start.2
  0.7 40.6 %project.1 = (bf16[2,8,128,128]{3,2,1,0:T(8,128)(2,1)S(1)}, bf16[8192,256]{1,0:T(8,128)(2,1)S(1)}, bf16[2048,256]{1,0:T(8,128)(2,1)S(1)}, f32[1,1024]{1,0:T(1,12...) custom-call(bf16[256,1280]{1,0:T(8,128)(2,1)} %bitcast.10, bf16[1,5120]{1,0:T(2,128)(2,1)} %gain_hbm.1, ...), custom_call_target="tpu_custom_call" | custom-call | tf_op jit(solution)/shard_map/project/pallas_call | solution.py:334
  41.3 0.0 copy-done.2
  41.3 0.0 copy-done.1
  41.3 0.0 copy-done.3
  41.3 8.5 %attend.1 = (bf16[128,1024]{1,0:T(8,128)(2,1)S(1)}, f32[1,1]{1,0:T(1,128)}, f32[1,1024]{1,0:T(1,128)S(1)}, f32[1,1024]{1,0:T(1,128)S(1)}, f32[128,1024]{1,0:T(8,128)S(1)}) custom-call(s32[1,4]{1,0:T(1,128)S(1)} %copy-done.1, s32[1,4]{1,0:T(1,128)S(1)} %copy-done.2, s32[16]{0:T(128)S(1)} %bitcast.13, bf16[2,8,128,128]{3,2,1,0:T(8,128)(2,1)S(1)} %get-tuple-element.13.q, ...), custom_call_target="tpu_custom_call" | custom-call | tf_op jit(solution)/shard_map/attend/pallas_call | solution.py:445
  49.8 0.0 slice-done
  49.8 0.0 copy-done
  49.8 0.0 slice-done.1
  49.9 0.0 slice-done.2
  49.9 34.9 %output.1 = bf16[256,1280]{1,0:T(8,128)(2,1)S(1)} custom-call(s32[1,4]{1,0:T(1,128)S(1)} %copy-done.1, s32[1,4]{1,0:T(1,128)S(1)} %copy-done.2, bf16[128,1024]{1,0:T(8,128)(2,1)S(1)} %get-tuple-element.19.att0, bf16[256,1280]{1,0:T(8,128)(2,1)S(1)} %bitcast.11, bf16[1024,5120]{1,0:T(8,128)(2,1)S(1)} %bitcast.9, ...), custom_call_target="tpu_custom_call" | custom-call | tf_op jit(solution)/shard_map/output/pallas_call | solution.py:635
  84.8 0.8 copy.12
  (1 shorter events, 0.0 us)
Async XLA Ops:
  0.6 40.7 %copy-start.2 = (s32[1,4]{1,0:T(1,128)S(1)}, s32[1,4]{1,0:T(1,128)}, u32[]{:S(2)}) copy-start(s32[1,4]{1,0:T(1,128)} %row_len.5) | copy-start | bytes 52
  0.6 40.7 %copy-start.1 = (s32[1,4]{1,0:T(1,128)S(1)}, s32[1,4]{1,0:T(1,128)}, u32[]{:S(2)}) copy-start(s32[1,4]{1,0:T(1,128)} %cache_len.5) | copy-start | bytes 52
  0.7 40.7 %copy-start.3 = (s32[1,16,1]{1,2,0:T(1,128)S(1)}, s32[1,16,1]{1,2,0:T(1,128)}, u32[]{:S(2)}) copy-start(s32[1,16,1]{1,2,0:T(1,128)} %param.17) | copy-start | bytes 196
  0.7 49.2 %slice-start = ((s8[10485760]{0:T(1024)(128)(4,1)}), s8[4194304]{0:T(1024)(128)(4,1)S(1)}, s32[]{:S(2)}) async-start(s8[10485760]{0:T(1024)(128)(4,1)} %bitcast.7), calls=%async_computation | async-start | bytes 8388608
  0.7 49.2 %copy-start = (bf16[1,256,1280]{2,1,0:T(8,128)(2,1)S(1)}, bf16[1,256,1280]{2,1,0:T(8,128)(2,1)}, u32[]{:S(2)}) copy-start(bf16[1,256,1280]{2,1,0:T(8,128)(2,1)} %param.9) | copy-start | bytes 1966084
  0.7 49.2 %slice-start.1 = ((s8[10485760]{0:T(1024)(128)(4,1)}), s8[4194304]{0:T(1024)(128)(4,1)S(1)}, s32[]{:S(2)}) async-start(s8[10485760]{0:T(1024)(128)(4,1)} %bitcast.7), calls=%async_computation.1 | async-start | bytes 8388608
  0.7 49.2 %slice-start.2 = ((s8[10485760]{0:T(1024)(128)(4,1)}), s8[2097152]{0:T(1024)(128)(4,1)S(1)}, s32[]{:S(2)}) async-start(s8[10485760]{0:T(1024)(128)(4,1)} %bitcast.7), calls=%async_computation.2 | async-start | bytes 4194304
